TPU v7x, 32 devices: a whole 2x2x4 slice. The times are simulated.
32 devices in a mesh: groups: 2 (over y), leaf: 4 (over z), sub: 2 (over x), rep: 2 (over core).
Axes of the slice: x: 2, y: 2, z: 4, core: 2. Of those that a mesh axis runs over, the one named last changes fastest.
Arguments:
- vectors: bfloat16 [16, 131072], P(None, ('groups', 'leaf', 'sub', 'rep')), parts along dimension 1, may hold values from -6 to 6
- positions: float32 [3, 131072], P(None, ('groups', 'leaf', 'sub', 'rep')), parts along dimension 1, may hold values from 0 to 65, as said below
- leaf_bases: bfloat16 [512, 64, 256], P(('groups', 'leaf', 'sub', 'rep')), parts along dimension 0, may hold values from -0.375 to 0.375
- low_pairs: bfloat16 [480, 64, 128], P(('groups', 'leaf', 'sub', 'rep')), parts along dimension 0, may hold values from -0.625 to 0.625
- low_tiles: bfloat16 [960, 64, 256], P(('groups', 'leaf', 'sub', 'rep')), parts along dimension 0, may hold values from -0.375 to 0.375
- low_lists: int32 [960, 4], P(('groups', 'leaf', 'sub', 'rep')), parts along dimension 0, may hold values from -3 to 3, as said below
- top_pairs: bfloat16 [32, 2, 64, 128], P(('groups', 'leaf', 'sub', 'rep')), parts along dimension 0, may hold values from -0.625 to 0.625
- top_tiles: bfloat16 [32, 3, 64, 256], P(('groups', 'leaf', 'sub', 'rep')), parts along dimension 0, may hold values from -0.375 to 0.375
- top_lists: int32 [32, 3, 4], P(('groups', 'leaf', 'sub', 'rep')), parts along dimension 0, may hold values from -3 to 3, as said below
Outputs:
- first_product: bfloat16 [16, 131072], P(None, ('groups', 'leaf', 'sub', 'rep')), parts along dimension 1
- second_product: bfloat16 [16, 131072], P(None, ('groups', 'leaf', 'sub', 'rep')), parts along dimension 1
There are 2 independent parts, one for each index of `groups`. A program takes and returns all parts, laid end to end along the dimension named above; each array names one. Nothing has to cross between parts.
Inputs may be any that keep to these rules, and one draw needn't show every extreme that they name: `positions`: point p lies in the box of its leaf l = p // 256: first coordinate (along the track) in [l / 4, l / 4 + 1), the other two in [0, 1). `low_lists`: a cluster whose index within its level is even lists -2, 2, 3 and 0, each once, in some order; one whose index is odd lists -3, -2, 2 and 0, each once, in some order. `top_lists`: a cluster whose index within its level is even lists -2, 2, 3 and 0, each once, in some order; one whose index is odd lists -3, -2, 2 and 0, each once, in some order.
All inputs are finite; a program needn't handle non-finite values.
Results may differ from a plain program's by a relative error of at most 0.015.
Values may be sent and summed in bfloat16 or wider, within the bound.
A program may use at most 64 MiB of HBM per device.

v0:
```python
import jax
import jax.numpy as jnp
from jax import lax
from jax.sharding import PartitionSpec as P

AMPLITUDE = 0.15
SLOPE = 1.7320508075688772 / 0.3
OFFSETS = (-3, -2, 2, 3)


def from_behind(value, axis, steps):
    count = lax.axis_size(axis)
    leading, last = (max(0, -steps), min(count, count - steps))
    return lax.ppermute(value, axis, [(source, source + steps) for source in range(leading, last)])


def extended_2(x, sides, width):
    for axis, dim in sides:
        peers, length = (lax.axis_size(axis), x.shape[dim])
        up = [(i, (i + 1) % peers) for i in range(peers - 1)]
        down = [(j, i) for i, j in up]
        last = lax.slice_in_dim(x, length - width, length, axis=dim)
        leading = lax.slice_in_dim(x, 0, width, axis=dim)
        before = lax.ppermute(last, axis, up)
        after = lax.ppermute(leading, axis, down)
        x = jnp.concatenate([before, x, after], axis=dim)
    return x


def kernel_block(targets, sources):
    square = jnp.zeros((targets.shape[1], sources.shape[1]), targets.dtype)
    for coord_index in range(3):
        delta = targets[coord_index][:, None] - sources[coord_index][None, :]
        square = square + delta * delta
    distance = jnp.sqrt(square)
    return AMPLITUDE * (1.0 + SLOPE * distance) * jnp.exp(-SLOPE * distance)


def near_field(ext_values, ext_coords, leaf_count, leaf_points):
    rows = 2 * leaf_points
    width = 8 * leaf_points
    row_leaf = jnp.arange(rows, dtype=jnp.int32) // leaf_points
    col_leaf = jnp.arange(width, dtype=jnp.int32) // leaf_points
    keep = jnp.abs(row_leaf[:, None] + 3 - col_leaf[None, :]) <= 3

    def one_block(block_index):
        start = block_index * rows
        targets = lax.dynamic_slice_in_dim(ext_coords, start + 3 * leaf_points, rows, 1)
        sources = lax.dynamic_slice_in_dim(ext_coords, start, width, 1)
        weights = jnp.where(keep, kernel_block(targets, sources), 0.0).astype(jnp.bfloat16)
        inputs = lax.dynamic_slice_in_dim(ext_values, start, width, 1)
        return lax.dot_general(
            inputs, weights, (((1,), (1,)), ((), ())), preferred_element_type=jnp.float32
        )

    blocks = lax.map(one_block, jnp.arange(leaf_count // 2, dtype=jnp.int32))
    return jnp.transpose(blocks, (1, 0, 2)).reshape(ext_values.shape[0], leaf_count * leaf_points)


def partner_product(tiles, lists, slices):
    picked = []
    for slot in range(lists.shape[1]):
        chosen = jnp.zeros_like(slices[OFFSETS[0]])
        for offset in OFFSETS:
            chosen = jnp.where((lists[:, slot] == offset)[:, None, None], slices[offset], chosen)
        picked.append(chosen)
    joined = jnp.stack(picked, axis=2)
    joined = joined.reshape(joined.shape[0], joined.shape[1], -1)
    return jnp.einsum("irq,ivq->ivr", tiles, joined, preferred_element_type=jnp.float32)


def join_children(child):
    parents = child.shape[0] // 2
    shaped = child.reshape(parents, 2, child.shape[1], child.shape[2])
    return jnp.transpose(shaped, (0, 2, 1, 3)).reshape(parents, child.shape[1], 2 * child.shape[2])


def split_children(spread):
    parents, columns, doubled = spread.shape
    shaped = spread.reshape(parents, columns, 2, doubled // 2)
    return jnp.transpose(shaped, (0, 2, 1, 3)).reshape(2 * parents, columns, doubled // 2)


def lift(pair, joined):
    return jnp.einsum("irq,ivq->ivr", pair, joined, preferred_element_type=jnp.float32).astype(
        jnp.bfloat16
    )


def lower(pair, field):
    return jnp.einsum("irq,ivr->ivq", pair, field, preferred_element_type=jnp.float32).astype(
        jnp.bfloat16
    )


def flatten(array):
    return array.reshape(array.shape[0], -1)


def whole_extend(coeffs, amounts):
    stacked = jnp.concatenate(coeffs[: len(amounts)], axis=0)
    moved = {}
    for distance in (1, 2, -1, -2):
        moved[distance] = from_behind(flatten(stacked), ("leaf", "sub", "rep"), distance).reshape(
            stacked.shape
        )
    result = []
    start = 0
    for height in range(len(amounts)):
        amount = amounts[height]
        stop = start + amount
        padded = jnp.concatenate(
            [
                moved[2][start:stop],
                moved[1][start:stop],
                coeffs[height],
                moved[-1][start:stop],
                moved[-2][start:stop],
            ],
            axis=0,
        )
        centre = 2 * amount
        result.append(
            {offset: padded[centre + offset : centre + offset + amount] for offset in OFFSETS}
        )
        start = stop
    return result


def level_partners(top_coeffs):
    result = []
    for height in range(len(top_coeffs)):
        stride = 1 << height
        own = top_coeffs[height]
        slices = {}
        for offset in OFFSETS:
            slices[offset] = from_behind(
                flatten(own), ("leaf", "sub", "rep"), -offset * stride
            ).reshape(own.shape)
        result.append(slices)
    return result


def apply_once(
    vectors,
    ext_coords,
    leaf_bases,
    low_pairs,
    low_tiles,
    low_lists,
    top_pairs,
    top_tiles,
    top_lists,
):
    shards = lax.axis_size(("leaf", "sub", "rep"))
    own_index = lax.axis_index(("leaf", "sub", "rep"))
    leaf_count, basis_rank, leaf_points = leaf_bases.shape
    columns = vectors.shape[0]
    ext_values = extended_2(vectors, ((("leaf", "sub", "rep"), 1),), 3 * leaf_points)
    near = near_field(ext_values, ext_coords, leaf_count, leaf_points)
    leaf_values = vectors.reshape(columns, leaf_count, leaf_points)
    coeffs = [
        jnp.einsum(
            "lrp,vlp->lvr", leaf_bases, leaf_values, preferred_element_type=jnp.float32
        ).astype(jnp.bfloat16)
    ]
    local_levels = leaf_count.bit_length() - 1
    amounts = [leaf_count >> height for height in range(local_levels)]
    starts = [sum(amounts[:height]) for height in range(local_levels)]
    pair_starts = [sum(amounts[1 : height + 1]) for height in range(local_levels)]
    for height in range(local_levels):
        parents = amounts[height] // 2
        pair = low_pairs[pair_starts[height] : pair_starts[height] + parents]
        coeffs.append(lift(pair, join_children(coeffs[height])))
    extended = whole_extend(coeffs, amounts)
    low_terms = []
    for height in range(local_levels):
        stop = starts[height] + amounts[height]
        low_terms.append(
            partner_product(
                low_tiles[starts[height] : stop], low_lists[starts[height] : stop], extended[height]
            )
        )
    top_count = shards.bit_length() - 2
    top_coeffs = [coeffs[local_levels]]
    first_level = 0
    for height in range(first_level, top_count - 1):
        stride = 1 << height
        own = top_coeffs[height]
        right = from_behind(flatten(own), ("leaf", "sub", "rep"), -stride).reshape(own.shape)
        top_coeffs.append(lift(top_pairs[:, height], jnp.concatenate([own, right], axis=2)))
    top_slices = level_partners(top_coeffs)
    top_terms = [
        partner_product(top_tiles[:, height], top_lists[:, height], top_slices[height])
        for height in range(top_count)
    ]
    field = top_terms[top_count - 1].astype(jnp.bfloat16)
    for height in range(top_count - 2, first_level - 1, -1):
        stride = 1 << height
        spread = lower(top_pairs[:, height], field)
        left_part = spread[:, :, :basis_rank]
        right_part = spread[:, :, basis_rank:]
        moved = from_behind(flatten(right_part), ("leaf", "sub", "rep"), stride).reshape(
            right_part.shape
        )
        share = jnp.where(own_index % (2 * stride) == 0, left_part, moved)
        field = (top_terms[height] + share.astype(jnp.float32)).astype(jnp.bfloat16)
    for height in range(local_levels - 1, -1, -1):
        parents = amounts[height] // 2
        pair = low_pairs[pair_starts[height] : pair_starts[height] + parents]
        spread = lower(pair, field)
        field = (low_terms[height] + split_children(spread).astype(jnp.float32)).astype(
            jnp.bfloat16
        )
    far = jnp.einsum("lrp,lvr->vlp", leaf_bases, field, preferred_element_type=jnp.float32)
    return (near + far.reshape(columns, leaf_count * leaf_points)).astype(jnp.bfloat16)


def body(
    vectors, positions, leaf_bases, low_pairs, low_tiles, low_lists, top_pairs, top_tiles, top_lists
):
    ext_coords = extended_2(positions, ((("leaf", "sub", "rep"), 1),), 3 * leaf_bases.shape[2])
    first_product = apply_once(
        vectors,
        ext_coords,
        leaf_bases,
        low_pairs,
        low_tiles,
        low_lists,
        top_pairs,
        top_tiles,
        top_lists,
    )
    second_product = apply_once(
        first_product,
        ext_coords,
        leaf_bases,
        low_pairs,
        low_tiles,
        low_lists,
        top_pairs,
        top_tiles,
        top_lists,
    )
    return (first_product, second_product)


def solution(mesh):
    placed = (
        P(None, ("groups", "leaf", "sub", "rep")),
        P(None, ("groups", "leaf", "sub", "rep")),
        P(("groups", "leaf", "sub", "rep"), None, None),
        P(("groups", "leaf", "sub", "rep"), None, None),
        P(("groups", "leaf", "sub", "rep"), None, None),
        P(("groups", "leaf", "sub", "rep"), None),
        P(("groups", "leaf", "sub", "rep"), None, None, None),
        P(("groups", "leaf", "sub", "rep"), None, None, None),
        P(("groups", "leaf", "sub", "rep"), None, None),
    )
    return jax.shard_map(
        body,
        mesh=mesh,
        in_specs=placed,
        out_specs=(
            P(None, ("groups", "leaf", "sub", "rep")),
            P(None, ("groups", "leaf", "sub", "rep")),
        ),
        check_vma=False,
    )
```

profile of v0, /device:TPU:0, one launch (start us, length us, event | category | flops | bytes accessed | tf_op | source)
XLA Modules:
  0.0 287.1 jit_solution(9107740257336704323)
XLA Ops:
  5.2 1.3 collective-permute-start.12
  6.5 5.5 %collective-permute-start.10 = (bf16[1,1024]{1,0:T(2,128)(2,1)S(1)}, bf16[1,1024]{1,0:T(2,128)(2,1)S(1)}, u32[]{:S(2)}, u32[]{:S(2)}) collective-permute-start(bf16[1,1024]{1,0:T(2,128)(2,1)S(1)} %reshape.2677), channel_id=1, source_target_pairs={{0,2},{1,3},{2,4},{3,5},{4,6},{5,7},{6,8},{7,9},{8,10},{9,11},{10,... | collective-permute-start | bytes 6152 | tf_op jit(solution)/shard_map/ppermute | solution.py:14
  11.9 3.3 %collective-permute-start.11 = (bf16[1,1024]{1,0:T(2,128)(2,1)S(1)}, bf16[1,1024]{1,0:T(2,128)(2,1)S(1)}, u32[]{:S(2)}, u32[]{:S(2)}) collective-permute-start(bf16[1,1024]{1,0:T(2,128)(2,1)S(1)} %reshape.2677), channel_id=1, source_target_pairs={{0,3},{1,4},{2,5},{3,6},{4,7},{5,8},{6,9},{7,10},{8,11},{9,12},{10... | collective-permute-start | bytes 6152 | tf_op jit(solution)/shard_map/ppermute | solution.py:14
  15.2 1.3 collective-permute-start.8
  16.5 1.3 collective-permute-start.9
  51.2 1.3 collective-permute-start.4
  52.9 1.3 collective-permute-start.17
  54.2 1.3 collective-permute-start.13
  55.5 1.3 collective-permute-start.14
  56.8 8.8 %collective-permute-start.15 = (bf16[1,1024]{1,0:T(2,128)(2,1)S(1)}, bf16[1,1024]{1,0:T(2,128)(2,1)S(1)}, u32[]{:S(2)}, u32[]{:S(2)}) collective-permute-start(bf16[1,1024]{1,0:T(2,128)(2,1)S(1)} %reshape.2683), channel_id=1, source_target_pairs={{0,4},{1,5},{2,6},{3,7},{4,8},{5,9},{6,10},{7,11},{8,12},{9,13},{1... | collective-permute-start | bytes 6152 | tf_op jit(solution)/shard_map/ppermute | solution.py:14
  66.1 6.0 %collective-permute-start.16 = (bf16[1,1024]{1,0:T(2,128)(2,1)S(1)}, bf16[1,1024]{1,0:T(2,128)(2,1)S(1)}, u32[]{:S(2)}, u32[]{:S(2)}) collective-permute-start(bf16[1,1024]{1,0:T(2,128)(2,1)S(1)} %reshape.2683), channel_id=1, source_target_pairs={{0,6},{1,7},{2,8},{3,9},{4,10},{5,11},{6,12},{7,13},{8,14},{9,15},... | collective-permute-start | bytes 6152 | tf_op jit(solution)/shard_map/ppermute | solution.py:14
  72.5 1.3 collective-permute-start.18
  73.8 1.3 collective-permute-start.19
  75.1 5.4 %collective-permute-start.20 = (bf16[1,1024]{1,0:T(2,128)(2,1)S(1)}, bf16[1,1024]{1,0:T(2,128)(2,1)S(1)}, u32[]{:S(2)}, u32[]{:S(2)}) collective-permute-start(bf16[1,1024]{1,0:T(2,128)(2,1)S(1)} %reshape.2689), channel_id=1, source_target_pairs={{0,8},{1,9},{2,10},{3,11},{4,12},{5,13},{6,14},{7,15},{16,24},{17,... | collective-permute-start | bytes 6152 | tf_op jit(solution)/shard_map/ppermute | solution.py:14
  80.6 2.2 collective-permute-start.21
  83.2 1.3 collective-permute-start.5
  84.5 1.3 collective-permute-start.6
  85.8 5.3 %collective-permute-start.2 = (f32[3,768]{1,0:T(4,128)S(1)}, f32[3,768]{1,0:T(4,128)S(1)}, u32[]{:S(2)}, u32[]{:S(2)}) collective-permute-start(f32[3,768]{1,0:T(4,128)S(1)} %get-tuple-element.305), channel_id=1, source_target_pairs={{0,1},{1,2},{2,3},{3,4},{4,5},{5,6},{6,7},{7,8},{8,9},{9,10},{10,1... | collective-permute-start | bytes 27656 | tf_op jit(solution)/shard_map/ppermute | solution.py:24
  92.0 4.3 %collective-permute-start.22 = (bf16[1,1024]{1,0:T(2,128)(2,1)S(1)}, bf16[1,1024]{1,0:T(2,128)(2,1)S(1)}, u32[]{:S(2)}, u32[]{:S(2)}) collective-permute-start(bf16[1,1024]{1,0:T(2,128)(2,1)S(1)} %reshape.2692), channel_id=1, source_target_pairs={{0,2},{1,3},{2,4},{3,5},{4,6},{5,7},{6,8},{7,9},{8,10},{9,11},{10,... | collective-permute-start | bytes 6152 | tf_op jit(solution)/shard_map/ppermute | solution.py:14
  97.6 1.3 collective-permute-start.3
  99.4 3.0 %collective-permute-start = (bf16[16,768]{1,0:T(8,128)(2,1)S(1)}, bf16[16,768]{1,0:T(8,128)(2,1)S(1)}, u32[]{:S(2)}, u32[]{:S(2)}) collective-permute-start(bf16[16,768]{1,0:T(8,128)(2,1)S(1)} %get-tuple-element.296), channel_id=1, source_target_pairs={{0,1},{1,2},{2,3},{3,4},{4,5},{5,6},{6,7},{7,8},{8,9},{9,10},{10,1... | collective-permute-start | bytes 73736 | tf_op jit(solution)/shard_map/ppermute | solution.py:24
  102.5 3.8 %collective-permute-start.23 = (bf16[1,1024]{1,0:T(2,128)(2,1)S(1)}, bf16[1,1024]{1,0:T(2,128)(2,1)S(1)}, u32[]{:S(2)}, u32[]{:S(2)}) collective-permute-start(bf16[1,1024]{1,0:T(2,128)(2,1)S(1)} %reshape.2695), channel_id=1, source_target_pairs={{0,1},{1,2},{2,3},{3,4},{4,5},{5,6},{6,7},{7,8},{8,9},{9,10},{10,1... | collective-permute-start | bytes 6152 | tf_op jit(solution)/shard_map/ppermute | solution.py:14
  107.1 1.3 collective-permute-start.1
  108.9 5.8 %collective-permute-start.7 = (bf16[30,1024]{1,0:T(8,128)(2,1)S(1)}, bf16[30,1024]{1,0:T(8,128)(2,1)}, u32[]{:S(2)}, u32[]{:S(2)}) collective-permute-start(bf16[30,1024]{1,0:T(8,128)(2,1)S(1)} %reshape.2669), channel_id=1, source_target_pairs={{0,2},{1,3},{2,4},{3,5},{4,6},{5,7},{6,8},{7,9},{8,10},{9,11},{10,... | collective-permute-start | bytes 184328 | tf_op jit(solution)/shard_map/ppermute | solution.py:14
  114.7 43.0 %while.26 = (s32[]{:T(128)}, f32[8,16,512]{2,1,0:T(8,128)S(1)}, s32[8]{0:T(128)S(1)}, bf16[16,5632]{1,0:T(8,128)(2,1)S(1)}, f32[3,5632]{1,0:T(4,128)S(1)}, /*ind...) while((s32[]{:T(128)}, f32[8,16,512]{2,1,0:T(8,128)S(1)}, ...), condition=%wide.region_1.2_spmd.clone, body=%wide.region_0.1_spmd.clone.sunk | while | flops 52428812 | bytes 201005 | solution.py:56
  116.2 3.9 %fusion.261 = f32[8,16,512]{2,1,0:T(8,128)S(1)} fusion(f32[8,16,512]{2,1,0:T(8,128)S(1)} %get-tuple-element.539, s32[]{:T(128)} %get-tuple-element.538, s32[2048]{0:T(1024)S(1)} %get-tuple-element.558, s32[512]{0:T(512)S(1)} %get-tuple-element.559, f32[2048]{0:T(1024)S(1)} %bitcast.530, f32[512]{0:T(512)S(1)} %bitcast.542, f32[2048]{0:T(1024)S(1)} %bitcast.529, ...), kind=kOutput, calls=%fused_computation.6.clone.1 | convolution fusion | flops 52428800 | bytes 139272 | tf_op jit(solution)/shard_map/while/body/eval_jaxpr/dot_general | solution.py:52
  121.5 3.9 %fusion.261 = f32[8,16,512]{2,1,0:T(8,128)S(1)} fusion(f32[8,16,512]{2,1,0:T(8,128)S(1)} %get-tuple-element.539, s32[]{:T(128)} %get-tuple-element.538, s32[2048]{0:T(1024)S(1)} %get-tuple-element.558, s32[512]{0:T(512)S(1)} %get-tuple-element.559, f32[2048]{0:T(1024)S(1)} %bitcast.530, f32[512]{0:T(512)S(1)} %bitcast.542, f32[2048]{0:T(1024)S(1)} %bitcast.529, ...), kind=kOutput, calls=%fused_computation.6.clone.1 | convolution fusion | flops 52428800 | bytes 139272 | tf_op jit(solution)/shard_map/while/body/eval_jaxpr/dot_general | solution.py:52
  126.9 3.9 %fusion.261 = f32[8,16,512]{2,1,0:T(8,128)S(1)} fusion(f32[8,16,512]{2,1,0:T(8,128)S(1)} %get-tuple-element.539, s32[]{:T(128)} %get-tuple-element.538, s32[2048]{0:T(1024)S(1)} %get-tuple-element.558, s32[512]{0:T(512)S(1)} %get-tuple-element.559, f32[2048]{0:T(1024)S(1)} %bitcast.530, f32[512]{0:T(512)S(1)} %bitcast.542, f32[2048]{0:T(1024)S(1)} %bitcast.529, ...), kind=kOutput, calls=%fused_computation.6.clone.1 | convolution fusion | flops 52428800 | bytes 139272 | tf_op jit(solution)/shard_map/while/body/eval_jaxpr/dot_general | solution.py:52
  132.3 3.9 %fusion.261 = f32[8,16,512]{2,1,0:T(8,128)S(1)} fusion(f32[8,16,512]{2,1,0:T(8,128)S(1)} %get-tuple-element.539, s32[]{:T(128)} %get-tuple-element.538, s32[2048]{0:T(1024)S(1)} %get-tuple-element.558, s32[512]{0:T(512)S(1)} %get-tuple-element.559, f32[2048]{0:T(1024)S(1)} %bitcast.530, f32[512]{0:T(512)S(1)} %bitcast.542, f32[2048]{0:T(1024)S(1)} %bitcast.529, ...), kind=kOutput, calls=%fused_computation.6.clone.1 | convolution fusion | flops 52428800 | bytes 139272 | tf_op jit(solution)/shard_map/while/body/eval_jaxpr/dot_general | solution.py:52
  137.6 3.9 %fusion.261 = f32[8,16,512]{2,1,0:T(8,128)S(1)} fusion(f32[8,16,512]{2,1,0:T(8,128)S(1)} %get-tuple-element.539, s32[]{:T(128)} %get-tuple-element.538, s32[2048]{0:T(1024)S(1)} %get-tuple-element.558, s32[512]{0:T(512)S(1)} %get-tuple-element.559, f32[2048]{0:T(1024)S(1)} %bitcast.530, f32[512]{0:T(512)S(1)} %bitcast.542, f32[2048]{0:T(1024)S(1)} %bitcast.529, ...), kind=kOutput, calls=%fused_computation.6.clone.1 | convolution fusion | flops 52428800 | bytes 139272 | tf_op jit(solution)/shard_map/while/body/eval_jaxpr/dot_general | solution.py:52
  143.0 3.9 %fusion.261 = f32[8,16,512]{2,1,0:T(8,128)S(1)} fusion(f32[8,16,512]{2,1,0:T(8,128)S(1)} %get-tuple-element.539, s32[]{:T(128)} %get-tuple-element.538, s32[2048]{0:T(1024)S(1)} %get-tuple-element.558, s32[512]{0:T(512)S(1)} %get-tuple-element.559, f32[2048]{0:T(1024)S(1)} %bitcast.530, f32[512]{0:T(512)S(1)} %bitcast.542, f32[2048]{0:T(1024)S(1)} %bitcast.529, ...), kind=kOutput, calls=%fused_computation.6.clone.1 | convolution fusion | flops 52428800 | bytes 139272 | tf_op jit(solution)/shard_map/while/body/eval_jaxpr/dot_general | solution.py:52
  148.4 3.9 %fusion.261 = f32[8,16,512]{2,1,0:T(8,128)S(1)} fusion(f32[8,16,512]{2,1,0:T(8,128)S(1)} %get-tuple-element.539, s32[]{:T(128)} %get-tuple-element.538, s32[2048]{0:T(1024)S(1)} %get-tuple-element.558, s32[512]{0:T(512)S(1)} %get-tuple-element.559, f32[2048]{0:T(1024)S(1)} %bitcast.530, f32[512]{0:T(512)S(1)} %bitcast.542, f32[2048]{0:T(1024)S(1)} %bitcast.529, ...), kind=kOutput, calls=%fused_computation.6.clone.1 | convolution fusion | flops 52428800 | bytes 139272 | tf_op jit(solution)/shard_map/while/body/eval_jaxpr/dot_general | solution.py:52
  153.7 3.9 %fusion.261 = f32[8,16,512]{2,1,0:T(8,128)S(1)} fusion(f32[8,16,512]{2,1,0:T(8,128)S(1)} %get-tuple-element.539, s32[]{:T(128)} %get-tuple-element.538, s32[2048]{0:T(1024)S(1)} %get-tuple-element.558, s32[512]{0:T(512)S(1)} %get-tuple-element.559, f32[2048]{0:T(1024)S(1)} %bitcast.530, f32[512]{0:T(512)S(1)} %bitcast.542, f32[2048]{0:T(1024)S(1)} %bitcast.529, ...), kind=kOutput, calls=%fused_computation.6.clone.1 | convolution fusion | flops 52428800 | bytes 139272 | tf_op jit(solution)/shard_map/while/body/eval_jaxpr/dot_general | solution.py:52
  165.8 1.3 collective-permute-start.34
  167.1 1.3 collective-permute-start.30
  168.4 1.3 collective-permute-start.31
  169.7 5.6 %collective-permute-start.32 = (bf16[1,1024]{1,0:T(2,128)(2,1)S(1)}, bf16[1,1024]{1,0:T(2,128)(2,1)S(1)}, u32[]{:S(2)}, u32[]{:S(2)}) collective-permute-start(bf16[1,1024]{1,0:T(2,128)(2,1)S(1)} %reshape.2714), channel_id=1, source_target_pairs={{0,2},{1,3},{2,4},{3,5},{4,6},{5,7},{6,8},{7,9},{8,10},{9,11},{10,... | collective-permute-start | bytes 6152 | tf_op jit(solution)/shard_map/ppermute | solution.py:14
  175.3 5.2 %collective-permute-start.33 = (bf16[1,1024]{1,0:T(2,128)(2,1)S(1)}, bf16[1,1024]{1,0:T(2,128)(2,1)S(1)}, u32[]{:S(2)}, u32[]{:S(2)}) collective-permute-start(bf16[1,1024]{1,0:T(2,128)(2,1)S(1)} %reshape.2714), channel_id=1, source_target_pairs={{0,3},{1,4},{2,5},{3,6},{4,7},{5,8},{6,9},{7,10},{8,11},{9,12},{10... | collective-permute-start | bytes 6152 | tf_op jit(solution)/shard_map/ppermute | solution.py:14
  180.8 1.3 collective-permute-start.26
  182.5 1.3 collective-permute-start.39
  183.8 1.3 collective-permute-start.35
  185.1 1.3 collective-permute-start.36
  186.4 7.8 %collective-permute-start.37 = (bf16[1,1024]{1,0:T(2,128)(2,1)S(1)}, bf16[1,1024]{1,0:T(2,128)(2,1)S(1)}, u32[]{:S(2)}, u32[]{:S(2)}) collective-permute-start(bf16[1,1024]{1,0:T(2,128)(2,1)S(1)} %reshape.2718), channel_id=1, source_target_pairs={{0,4},{1,5},{2,6},{3,7},{4,8},{5,9},{6,10},{7,11},{8,12},{9,13},{1... | collective-permute-start | bytes 6152 | tf_op jit(solution)/shard_map/ppermute | solution.py:14
  194.6 5.7 %collective-permute-start.38 = (bf16[1,1024]{1,0:T(2,128)(2,1)S(1)}, bf16[1,1024]{1,0:T(2,128)(2,1)S(1)}, u32[]{:S(2)}, u32[]{:S(2)}) collective-permute-start(bf16[1,1024]{1,0:T(2,128)(2,1)S(1)} %reshape.2718), channel_id=1, source_target_pairs={{0,6},{1,7},{2,8},{3,9},{4,10},{5,11},{6,12},{7,13},{8,14},{9,15},... | collective-permute-start | bytes 6152 | tf_op jit(solution)/shard_map/ppermute | solution.py:14
  200.7 1.3 collective-permute-start.40
  202.0 1.3 collective-permute-start.41
  203.3 5.4 %collective-permute-start.42 = (bf16[1,1024]{1,0:T(2,128)(2,1)S(1)}, bf16[1,1024]{1,0:T(2,128)(2,1)S(1)}, u32[]{:S(2)}, u32[]{:S(2)}) collective-permute-start(bf16[1,1024]{1,0:T(2,128)(2,1)S(1)} %reshape.2722), channel_id=1, source_target_pairs={{0,8},{1,9},{2,10},{3,11},{4,12},{5,13},{6,14},{7,15},{16,24},{17,... | collective-permute-start | bytes 6152 | tf_op jit(solution)/shard_map/ppermute | solution.py:14
  208.8 2.2 collective-permute-start.43
  211.4 1.3 collective-permute-start.28
  212.7 1.3 collective-permute-start.27
  214.0 5.3 %collective-permute-start.24 = (bf16[16,768]{1,0:T(8,128)(2,1)S(1)}, bf16[16,768]{1,0:T(8,128)(2,1)S(1)}, u32[]{:S(2)}, u32[]{:S(2)}) collective-permute-start(bf16[16,768]{1,0:T(8,128)(2,1)S(1)} %get-tuple-element.291), channel_id=1, source_target_pairs={{0,1},{1,2},{2,3},{3,4},{4,5},{5,6},{6,7},{7,8},{8,9},{9,10},{10,1... | collective-permute-start | bytes 73736 | tf_op jit(solution)/shard_map/ppermute | solution.py:24
  220.2 4.5 %collective-permute-start.44 = (bf16[1,1024]{1,0:T(2,128)(2,1)S(1)}, bf16[1,1024]{1,0:T(2,128)(2,1)S(1)}, u32[]{:S(2)}, u32[]{:S(2)}) collective-permute-start(bf16[1,1024]{1,0:T(2,128)(2,1)S(1)} %reshape.2724), channel_id=1, source_target_pairs={{0,2},{1,3},{2,4},{3,5},{4,6},{5,7},{6,8},{7,9},{8,10},{9,11},{10,... | collective-permute-start | bytes 6152 | tf_op jit(solution)/shard_map/ppermute | solution.py:14
  226.6 1.3 collective-permute-start.45
  228.7 1.3 collective-permute-start.25
  230.4 7.6 %collective-permute-start.29 = (bf16[30,1024]{1,0:T(8,128)(2,1)S(1)}, bf16[30,1024]{1,0:T(8,128)(2,1)S(1)}, u32[]{:S(2)}, u32[]{:S(2)}) collective-permute-start(bf16[30,1024]{1,0:T(8,128)(2,1)S(1)} %reshape.2707), channel_id=1, source_target_pairs={{0,2},{1,3},{2,4},{3,5},{4,6},{5,7},{6,8},{7,9},{8,10},{9,11},{10,... | collective-permute-start | bytes 184328 | tf_op jit(solution)/shard_map/ppermute | solution.py:14
  238.3 43.0 %while.27 = (s32[]{:T(128)}, f32[8,16,512]{2,1,0:T(8,128)S(1)}, s32[8]{0:T(128)S(1)}, bf16[16,5632]{1,0:T(8,128)(2,1)S(1)}, f32[3,5632]{1,0:T(4,128)S(1)}, /*ind...) while((s32[]{:T(128)}, f32[8,16,512]{2,1,0:T(8,128)S(1)}, ...), condition=%wide.region_3.4_spmd.clone, body=%wide.region_2.3_spmd.clone.sunk | while | flops 52428812 | bytes 201005 | solution.py:56
  239.7 3.9 %fusion.263 = f32[8,16,512]{2,1,0:T(8,128)S(1)} fusion(f32[8,16,512]{2,1,0:T(8,128)S(1)} %get-tuple-element.584, s32[]{:T(128)} %get-tuple-element.583, s32[2048]{0:T(1024)S(1)} %get-tuple-element.603, s32[512]{0:T(512)S(1)} %get-tuple-element.604, f32[2048]{0:T(1024)S(1)} %bitcast.533, f32[512]{0:T(512)S(1)} %bitcast.545, f32[2048]{0:T(1024)S(1)} %bitcast.532, ...), kind=kOutput, calls=%fused_computation.21.clone.1 | convolution fusion | flops 52428800 | bytes 139272 | tf_op jit(solution)/shard_map/while/body/eval_jaxpr/dot_general | solution.py:52
  245.1 3.9 %fusion.263 = f32[8,16,512]{2,1,0:T(8,128)S(1)} fusion(f32[8,16,512]{2,1,0:T(8,128)S(1)} %get-tuple-element.584, s32[]{:T(128)} %get-tuple-element.583, s32[2048]{0:T(1024)S(1)} %get-tuple-element.603, s32[512]{0:T(512)S(1)} %get-tuple-element.604, f32[2048]{0:T(1024)S(1)} %bitcast.533, f32[512]{0:T(512)S(1)} %bitcast.545, f32[2048]{0:T(1024)S(1)} %bitcast.532, ...), kind=kOutput, calls=%fused_computation.21.clone.1 | convolution fusion | flops 52428800 | bytes 139272 | tf_op jit(solution)/shard_map/while/body/eval_jaxpr/dot_general | solution.py:52
  250.5 3.9 %fusion.263 = f32[8,16,512]{2,1,0:T(8,128)S(1)} fusion(f32[8,16,512]{2,1,0:T(8,128)S(1)} %get-tuple-element.584, s32[]{:T(128)} %get-tuple-element.583, s32[2048]{0:T(1024)S(1)} %get-tuple-element.603, s32[512]{0:T(512)S(1)} %get-tuple-element.604, f32[2048]{0:T(1024)S(1)} %bitcast.533, f32[512]{0:T(512)S(1)} %bitcast.545, f32[2048]{0:T(1024)S(1)} %bitcast.532, ...), kind=kOutput, calls=%fused_computation.21.clone.1 | convolution fusion | flops 52428800 | bytes 139272 | tf_op jit(solution)/shard_map/while/body/eval_jaxpr/dot_general | solution.py:52
  255.8 3.9 %fusion.263 = f32[8,16,512]{2,1,0:T(8,128)S(1)} fusion(f32[8,16,512]{2,1,0:T(8,128)S(1)} %get-tuple-element.584, s32[]{:T(128)} %get-tuple-element.583, s32[2048]{0:T(1024)S(1)} %get-tuple-element.603, s32[512]{0:T(512)S(1)} %get-tuple-element.604, f32[2048]{0:T(1024)S(1)} %bitcast.533, f32[512]{0:T(512)S(1)} %bitcast.545, f32[2048]{0:T(1024)S(1)} %bitcast.532, ...), kind=kOutput, calls=%fused_computation.21.clone.1 | convolution fusion | flops 52428800 | bytes 139272 | tf_op jit(solution)/shard_map/while/body/eval_jaxpr/dot_general | solution.py:52
  261.2 3.9 %fusion.263 = f32[8,16,512]{2,1,0:T(8,128)S(1)} fusion(f32[8,16,512]{2,1,0:T(8,128)S(1)} %get-tuple-element.584, s32[]{:T(128)} %get-tuple-element.583, s32[2048]{0:T(1024)S(1)} %get-tuple-element.603, s32[512]{0:T(512)S(1)} %get-tuple-element.604, f32[2048]{0:T(1024)S(1)} %bitcast.533, f32[512]{0:T(512)S(1)} %bitcast.545, f32[2048]{0:T(1024)S(1)} %bitcast.532, ...), kind=kOutput, calls=%fused_computation.21.clone.1 | convolution fusion | flops 52428800 | bytes 139272 | tf_op jit(solution)/shard_map/while/body/eval_jaxpr/dot_general | solution.py:52
  266.6 3.9 %fusion.263 = f32[8,16,512]{2,1,0:T(8,128)S(1)} fusion(f32[8,16,512]{2,1,0:T(8,128)S(1)} %get-tuple-element.584, s32[]{:T(128)} %get-tuple-element.583, s32[2048]{0:T(1024)S(1)} %get-tuple-element.603, s32[512]{0:T(512)S(1)} %get-tuple-element.604, f32[2048]{0:T(1024)S(1)} %bitcast.533, f32[512]{0:T(512)S(1)} %bitcast.545, f32[2048]{0:T(1024)S(1)} %bitcast.532, ...), kind=kOutput, calls=%fused_computation.21.clone.1 | convolution fusion | flops 52428800 | bytes 139272 | tf_op jit(solution)/shard_map/while/body/eval_jaxpr/dot_general | solution.py:52
  272.0 3.9 %fusion.263 = f32[8,16,512]{2,1,0:T(8,128)S(1)} fusion(f32[8,16,512]{2,1,0:T(8,128)S(1)} %get-tuple-element.584, s32[]{:T(128)} %get-tuple-element.583, s32[2048]{0:T(1024)S(1)} %get-tuple-element.603, s32[512]{0:T(512)S(1)} %get-tuple-element.604, f32[2048]{0:T(1024)S(1)} %bitcast.533, f32[512]{0:T(512)S(1)} %bitcast.545, f32[2048]{0:T(1024)S(1)} %bitcast.532, ...), kind=kOutput, calls=%fused_computation.21.clone.1 | convolution fusion | flops 52428800 | bytes 139272 | tf_op jit(solution)/shard_map/while/body/eval_jaxpr/dot_general | solution.py:52
  277.3 3.9 %fusion.263 = f32[8,16,512]{2,1,0:T(8,128)S(1)} fusion(f32[8,16,512]{2,1,0:T(8,128)S(1)} %get-tuple-element.584, s32[]{:T(128)} %get-tuple-element.583, s32[2048]{0:T(1024)S(1)} %get-tuple-element.603, s32[512]{0:T(512)S(1)} %get-tuple-element.604, f32[2048]{0:T(1024)S(1)} %bitcast.533, f32[512]{0:T(512)S(1)} %bitcast.545, f32[2048]{0:T(1024)S(1)} %bitcast.532, ...), kind=kOutput, calls=%fused_computation.21.clone.1 | convolution fusion | flops 52428800 | bytes 139272 | tf_op jit(solution)/shard_map/while/body/eval_jaxpr/dot_general | solution.py:52
  (439 shorter events, 44.4 us)
Async XLA Ops:
  3.0 49.6 %copy-start.5 = (bf16[1,2,64,128]{3,2,1,0:T(8,128)(2,1)S(1)}, bf16[1,2,64,128]{3,2,1,0:T(8,128)(2,1)}, u32[]{:S(2)}) copy-start(bf16[1,2,64,128]{3,2,1,0:T(8,128)(2,1)} %param.19) | copy-start | bytes 98308
  3.2 88.5 %copy-start.6 = (bf16[1,3,64,256]{3,2,1,0:T(8,128)(2,1)S(1)}, bf16[1,3,64,256]{3,2,1,0:T(8,128)(2,1)}, u32[]{:S(2)}) copy-start(bf16[1,3,64,256]{3,2,1,0:T(8,128)(2,1)} %param.20) | copy-start | bytes 294916
  5.2 46.0 %collective-permute-start.12 = (bf16[1,1024]{1,0:T(2,128)(2,1)S(1)}, bf16[1,1024]{1,0:T(2,128)(2,1)S(1)}, u32[]{:S(2)}, u32[]{:S(2)}) collective-permute-start(bf16[1,1024]{1,0:T(2,128)(2,1)S(1)} %reshape.2677), channel_id=1, source_target_pairs={{1,0},{2,1},{3,2},{4,3},{5,4},{6,5},{7,6},{8,7},{9,8},{10,9},{11,1... | collective-permute-start | bytes 6152 | tf_op jit(solution)/shard_map/ppermute | solution.py:14
  6.5 46.4 %collective-permute-start.10 = (bf16[1,1024]{1,0:T(2,128)(2,1)S(1)}, bf16[1,1024]{1,0:T(2,128)(2,1)S(1)}, u32[]{:S(2)}, u32[]{:S(2)}) collective-permute-start(bf16[1,1024]{1,0:T(2,128)(2,1)S(1)} %reshape.2677), channel_id=1, source_target_pairs={{0,2},{1,3},{2,4},{3,5},{4,6},{5,7},{6,8},{7,9},{8,10},{9,11},{10,... | collective-permute-start | bytes 6152 | tf_op jit(solution)/shard_map/ppermute | solution.py:14
  11.9 42.2 %collective-permute-start.11 = (bf16[1,1024]{1,0:T(2,128)(2,1)S(1)}, bf16[1,1024]{1,0:T(2,128)(2,1)S(1)}, u32[]{:S(2)}, u32[]{:S(2)}) collective-permute-start(bf16[1,1024]{1,0:T(2,128)(2,1)S(1)} %reshape.2677), channel_id=1, source_target_pairs={{0,3},{1,4},{2,5},{3,6},{4,7},{5,8},{6,9},{7,10},{8,11},{9,12},{10... | collective-permute-start | bytes 6152 | tf_op jit(solution)/shard_map/ppermute | solution.py:14
  15.2 40.3 %collective-permute-start.8 = (bf16[1,1024]{1,0:T(2,128)(2,1)S(1)}, bf16[1,1024]{1,0:T(2,128)(2,1)S(1)}, u32[]{:S(2)}, u32[]{:S(2)}) collective-permute-start(bf16[1,1024]{1,0:T(2,128)(2,1)S(1)} %reshape.2677), channel_id=1, source_target_pairs={{3,0},{4,1},{5,2},{6,3},{7,4},{8,5},{9,6},{10,7},{11,8},{12,9},{13... | collective-permute-start | bytes 6152 | tf_op jit(solution)/shard_map/ppermute | solution.py:14
  16.5 40.3 %collective-permute-start.9 = (bf16[1,1024]{1,0:T(2,128)(2,1)S(1)}, bf16[1,1024]{1,0:T(2,128)(2,1)S(1)}, u32[]{:S(2)}, u32[]{:S(2)}) collective-permute-start(bf16[1,1024]{1,0:T(2,128)(2,1)S(1)} %reshape.2677), channel_id=1, source_target_pairs={{2,0},{3,1},{4,2},{5,3},{6,4},{7,5},{8,6},{9,7},{10,8},{11,9},{12,... | collective-permute-start | bytes 6152 | tf_op jit(solution)/shard_map/ppermute | solution.py:14
  39.3 120.4 %copy-start.9 = (pred[2]{0:T(512)(128)(4,1)}, pred[2]{0:T(512)(128)(4,1)S(1)}, u32[]{:S(2)}) copy-start(pred[2]{0:T(512)(128)(4,1)S(1)} %get-tuple-element.341) | copy-start | bytes 10
  39.3 120.5 %copy-start.11 = (pred[2]{0:T(512)(128)(4,1)}, pred[2]{0:T(512)(128)(4,1)S(1)}, u32[]{:S(2)}) copy-start(pred[2]{0:T(512)(128)(4,1)S(1)} %get-tuple-element.342) | copy-start | bytes 10
  39.3 120.5 %copy-start.13 = (pred[2]{0:T(512)(128)(4,1)}, pred[2]{0:T(512)(128)(4,1)S(1)}, u32[]{:S(2)}) copy-start(pred[2]{0:T(512)(128)(4,1)S(1)} %get-tuple-element.343) | copy-start | bytes 10
  39.4 120.5 %copy-start.15 = (pred[2]{0:T(512)(128)(4,1)}, pred[2]{0:T(512)(128)(4,1)S(1)}, u32[]{:S(2)}) copy-start(pred[2]{0:T(512)(128)(4,1)S(1)} %get-tuple-element.344) | copy-start | bytes 10
  51.2 107.3 %collective-permute-start.4 = (bf16[30,1024]{1,0:T(8,128)(2,1)S(1)}, bf16[30,1024]{1,0:T(8,128)(2,1)S(1)}, u32[]{:S(2)}, u32[]{:S(2)}) collective-permute-start(bf16[30,1024]{1,0:T(8,128)(2,1)S(1)} %reshape.2669), channel_id=1, source_target_pairs={{1,0},{2,1},{3,2},{4,3},{5,4},{6,5},{7,6},{8,7},{9,8},{10,9},{11,1... | collective-permute-start | bytes 184328 | tf_op jit(solution)/shard_map/ppermute | solution.py:14
  52.9 13.2 %collective-permute-start.17 = (bf16[1,1024]{1,0:T(2,128)(2,1)S(1)}, bf16[1,1024]{1,0:T(2,128)(2,1)S(1)}, u32[]{:S(2)}, u32[]{:S(2)}) collective-permute-start(bf16[1,1024]{1,0:T(2,128)(2,1)S(1)} %reshape.2683), channel_id=1, source_target_pairs={{2,0},{3,1},{4,2},{5,3},{6,4},{7,5},{8,6},{9,7},{10,8},{11,9},{12,... | collective-permute-start | bytes 6152 | tf_op jit(solution)/shard_map/ppermute | solution.py:14
  54.2 18.3 %collective-permute-start.13 = (bf16[1,1024]{1,0:T(2,128)(2,1)S(1)}, bf16[1,1024]{1,0:T(2,128)(2,1)S(1)}, u32[]{:S(2)}, u32[]{:S(2)}) collective-permute-start(bf16[1,1024]{1,0:T(2,128)(2,1)S(1)} %reshape.2683), channel_id=1, source_target_pairs={{6,0},{7,1},{8,2},{9,3},{10,4},{11,5},{12,6},{13,7},{14,8},{15,9},... | collective-permute-start | bytes 6152 | tf_op jit(solution)/shard_map/ppermute | solution.py:14
  55.5 18.3 %collective-permute-start.14 = (bf16[1,1024]{1,0:T(2,128)(2,1)S(1)}, bf16[1,1024]{1,0:T(2,128)(2,1)S(1)}, u32[]{:S(2)}, u32[]{:S(2)}) collective-permute-start(bf16[1,1024]{1,0:T(2,128)(2,1)S(1)} %reshape.2683), channel_id=1, source_target_pairs={{4,0},{5,1},{6,2},{7,3},{8,4},{9,5},{10,6},{11,7},{12,8},{13,9},{1... | collective-permute-start | bytes 6152 | tf_op jit(solution)/shard_map/ppermute | solution.py:14
  56.8 18.3 %collective-permute-start.15 = (bf16[1,1024]{1,0:T(2,128)(2,1)S(1)}, bf16[1,1024]{1,0:T(2,128)(2,1)S(1)}, u32[]{:S(2)}, u32[]{:S(2)}) collective-permute-start(bf16[1,1024]{1,0:T(2,128)(2,1)S(1)} %reshape.2683), channel_id=1, source_target_pairs={{0,4},{1,5},{2,6},{3,7},{4,8},{5,9},{6,10},{7,11},{8,12},{9,13},{1... | collective-permute-start | bytes 6152 | tf_op jit(solution)/shard_map/ppermute | solution.py:14
  66.1 14.5 %collective-permute-start.16 = (bf16[1,1024]{1,0:T(2,128)(2,1)S(1)}, bf16[1,1024]{1,0:T(2,128)(2,1)S(1)}, u32[]{:S(2)}, u32[]{:S(2)}) collective-permute-start(bf16[1,1024]{1,0:T(2,128)(2,1)S(1)} %reshape.2683), channel_id=1, source_target_pairs={{0,6},{1,7},{2,8},{3,9},{4,10},{5,11},{6,12},{7,13},{8,14},{9,15},... | collective-permute-start | bytes 6152 | tf_op jit(solution)/shard_map/ppermute | solution.py:14
  72.5 10.7 %collective-permute-start.18 = (bf16[1,1024]{1,0:T(2,128)(2,1)S(1)}, bf16[1,1024]{1,0:T(2,128)(2,1)S(1)}, u32[]{:S(2)}, u32[]{:S(2)}) collective-permute-start(bf16[1,1024]{1,0:T(2,128)(2,1)S(1)} %reshape.2689), channel_id=1, source_target_pairs={{12,0},{13,1},{14,2},{15,3},{28,16},{29,17},{30,18},{31,19}} | collective-permute-start | bytes 6152 | tf_op jit(solution)/shard_map/ppermute | solution.py:14
  73.8 10.7 %collective-permute-start.19 = (bf16[1,1024]{1,0:T(2,128)(2,1)S(1)}, bf16[1,1024]{1,0:T(2,128)(2,1)S(1)}, u32[]{:S(2)}, u32[]{:S(2)}) collective-permute-start(bf16[1,1024]{1,0:T(2,128)(2,1)S(1)} %reshape.2689), channel_id=1, source_target_pairs={{8,0},{9,1},{10,2},{11,3},{12,4},{13,5},{14,6},{15,7},{24,16},{25,... | collective-permute-start | bytes 6152 | tf_op jit(solution)/shard_map/ppermute | solution.py:14
  75.1 10.7 %collective-permute-start.20 = (bf16[1,1024]{1,0:T(2,128)(2,1)S(1)}, bf16[1,1024]{1,0:T(2,128)(2,1)S(1)}, u32[]{:S(2)}, u32[]{:S(2)}) collective-permute-start(bf16[1,1024]{1,0:T(2,128)(2,1)S(1)} %reshape.2689), channel_id=1, source_target_pairs={{0,8},{1,9},{2,10},{3,11},{4,12},{5,13},{6,14},{7,15},{16,24},{17,... | collective-permute-start | bytes 6152 | tf_op jit(solution)/shard_map/ppermute | solution.py:14
  80.6 10.5 %collective-permute-start.21 = (bf16[1,1024]{1,0:T(2,128)(2,1)S(1)}, bf16[1,1024]{1,0:T(2,128)(2,1)S(1)}, u32[]{:S(2)}, u32[]{:S(2)}) collective-permute-start(bf16[1,1024]{1,0:T(2,128)(2,1)S(1)} %reshape.2689), channel_id=1, source_target_pairs={{0,12},{1,13},{2,14},{3,15},{16,28},{17,29},{18,30},{19,31}} | collective-permute-start | bytes 6152 | tf_op jit(solution)/shard_map/ppermute | solution.py:14
  83.2 75.4 %collective-permute-start.5 = (bf16[30,1024]{1,0:T(8,128)(2,1)S(1)}, bf16[30,1024]{1,0:T(8,128)(2,1)S(1)}, u32[]{:S(2)}, u32[]{:S(2)}) collective-permute-start(bf16[30,1024]{1,0:T(8,128)(2,1)S(1)} %reshape.2669), channel_id=1, source_target_pairs={{0,1},{1,2},{2,3},{3,4},{4,5},{5,6},{6,7},{7,8},{8,9},{9,10},{10,1... | collective-permute-start | bytes 184328 | tf_op jit(solution)/shard_map/ppermute | solution.py:14
  84.5 74.2 %collective-permute-start.6 = (bf16[30,1024]{1,0:T(8,128)(2,1)S(1)}, bf16[30,1024]{1,0:T(8,128)(2,1)S(1)}, u32[]{:S(2)}, u32[]{:S(2)}) collective-permute-start(bf16[30,1024]{1,0:T(8,128)(2,1)S(1)} %reshape.2669), channel_id=1, source_target_pairs={{2,0},{3,1},{4,2},{5,3},{6,4},{7,5},{8,6},{9,7},{10,8},{11,9},{12,... | collective-permute-start | bytes 184328 | tf_op jit(solution)/shard_map/ppermute | solution.py:14
  85.8 13.6 %collective-permute-start.2 = (f32[3,768]{1,0:T(4,128)S(1)}, f32[3,768]{1,0:T(4,128)S(1)}, u32[]{:S(2)}, u32[]{:S(2)}) collective-permute-start(f32[3,768]{1,0:T(4,128)S(1)} %get-tuple-element.305), channel_id=1, source_target_pairs={{0,1},{1,2},{2,3},{3,4},{4,5},{5,6},{6,7},{7,8},{8,9},{9,10},{10,1... | collective-permute-start | bytes 27656 | tf_op jit(solution)/shard_map/ppermute | solution.py:24
  92.0 5.6 %collective-permute-start.22 = (bf16[1,1024]{1,0:T(2,128)(2,1)S(1)}, bf16[1,1024]{1,0:T(2,128)(2,1)S(1)}, u32[]{:S(2)}, u32[]{:S(2)}) collective-permute-start(bf16[1,1024]{1,0:T(2,128)(2,1)S(1)} %reshape.2692), channel_id=1, source_target_pairs={{0,2},{1,3},{2,4},{3,5},{4,6},{5,7},{6,8},{7,9},{8,10},{9,11},{10,... | collective-permute-start | bytes 6152 | tf_op jit(solution)/shard_map/ppermute | solution.py:14
  97.6 4.9 %collective-permute-start.3 = (f32[3,768]{1,0:T(4,128)S(1)}, f32[3,768]{1,0:T(4,128)S(1)}, u32[]{:S(2)}, u32[]{:S(2)}) collective-permute-start(f32[3,768]{1,0:T(4,128)S(1)} %get-tuple-element.304), channel_id=1, source_target_pairs={{1,0},{2,1},{3,2},{4,3},{5,4},{6,5},{7,6},{8,7},{9,8},{10,9},{11,1... | collective-permute-start | bytes 27656 | tf_op jit(solution)/shard_map/ppermute | solution.py:25
  99.4 9.4 %collective-permute-start = (bf16[16,768]{1,0:T(8,128)(2,1)S(1)}, bf16[16,768]{1,0:T(8,128)(2,1)S(1)}, u32[]{:S(2)}, u32[]{:S(2)}) collective-permute-start(bf16[16,768]{1,0:T(8,128)(2,1)S(1)} %get-tuple-element.296), channel_id=1, source_target_pairs={{0,1},{1,2},{2,3},{3,4},{4,5},{5,6},{6,7},{7,8},{8,9},{9,10},{10,1... | collective-permute-start | bytes 73736 | tf_op jit(solution)/shard_map/ppermute | solution.py:24
  102.5 4.6 %collective-permute-start.23 = (bf16[1,1024]{1,0:T(2,128)(2,1)S(1)}, bf16[1,1024]{1,0:T(2,128)(2,1)S(1)}, u32[]{:S(2)}, u32[]{:S(2)}) collective-permute-start(bf16[1,1024]{1,0:T(2,128)(2,1)S(1)} %reshape.2695), channel_id=1, source_target_pairs={{0,1},{1,2},{2,3},{3,4},{4,5},{5,6},{6,7},{7,8},{8,9},{9,10},{10,1... | collective-permute-start | bytes 6152 | tf_op jit(solution)/shard_map/ppermute | solution.py:14
  107.1 7.5 %collective-permute-start.1 = (bf16[16,768]{1,0:T(8,128)(2,1)S(1)}, bf16[16,768]{1,0:T(8,128)(2,1)S(1)}, u32[]{:S(2)}, u32[]{:S(2)}) collective-permute-start(bf16[16,768]{1,0:T(8,128)(2,1)S(1)} %get-tuple-element.297), channel_id=1, source_target_pairs={{1,0},{2,1},{3,2},{4,3},{5,4},{6,5},{7,6},{8,7},{9,8},{10,9},{11,1... | collective-permute-start | bytes 73736 | tf_op jit(solution)/shard_map/ppermute | solution.py:25
  108.9 49.9 %collective-permute-start.7 = (bf16[30,1024]{1,0:T(8,128)(2,1)S(1)}, bf16[30,1024]{1,0:T(8,128)(2,1)}, u32[]{:S(2)}, u32[]{:S(2)}) collective-permute-start(bf16[30,1024]{1,0:T(8,128)(2,1)S(1)} %reshape.2669), channel_id=1, source_target_pairs={{0,2},{1,3},{2,4},{3,5},{4,6},{5,7},{6,8},{7,9},{8,10},{9,11},{10,... | collective-permute-start | bytes 184328 | tf_op jit(solution)/shard_map/ppermute | solution.py:14
  165.8 15.0 %collective-permute-start.34 = (bf16[1,1024]{1,0:T(2,128)(2,1)S(1)}, bf16[1,1024]{1,0:T(2,128)(2,1)S(1)}, u32[]{:S(2)}, u32[]{:S(2)}) collective-permute-start(bf16[1,1024]{1,0:T(2,128)(2,1)S(1)} %reshape.2714), channel_id=1, source_target_pairs={{1,0},{2,1},{3,2},{4,3},{5,4},{6,5},{7,6},{8,7},{9,8},{10,9},{11,1... | collective-permute-start | bytes 6152 | tf_op jit(solution)/shard_map/ppermute | solution.py:14
  167.1 15.4 %collective-permute-start.30 = (bf16[1,1024]{1,0:T(2,128)(2,1)S(1)}, bf16[1,1024]{1,0:T(2,128)(2,1)S(1)}, u32[]{:S(2)}, u32[]{:S(2)}) collective-permute-start(bf16[1,1024]{1,0:T(2,128)(2,1)S(1)} %reshape.2714), channel_id=1, source_target_pairs={{3,0},{4,1},{5,2},{6,3},{7,4},{8,5},{9,6},{10,7},{11,8},{12,9},{13... | collective-permute-start | bytes 6152 | tf_op jit(solution)/shard_map/ppermute | solution.py:14
  168.4 15.4 %collective-permute-start.31 = (bf16[1,1024]{1,0:T(2,128)(2,1)S(1)}, bf16[1,1024]{1,0:T(2,128)(2,1)S(1)}, u32[]{:S(2)}, u32[]{:S(2)}) collective-permute-start(bf16[1,1024]{1,0:T(2,128)(2,1)S(1)} %reshape.2714), channel_id=1, source_target_pairs={{2,0},{3,1},{4,2},{5,3},{6,4},{7,5},{8,6},{9,7},{10,8},{11,9},{12,... | collective-permute-start | bytes 6152 | tf_op jit(solution)/shard_map/ppermute | solution.py:14
  169.7 15.4 %collective-permute-start.32 = (bf16[1,1024]{1,0:T(2,128)(2,1)S(1)}, bf16[1,1024]{1,0:T(2,128)(2,1)S(1)}, u32[]{:S(2)}, u32[]{:S(2)}) collective-permute-start(bf16[1,1024]{1,0:T(2,128)(2,1)S(1)} %reshape.2714), channel_id=1, source_target_pairs={{0,2},{1,3},{2,4},{3,5},{4,6},{5,7},{6,8},{7,9},{8,10},{9,11},{10,... | collective-permute-start | bytes 6152 | tf_op jit(solution)/shard_map/ppermute | solution.py:14
  175.3 11.1 %collective-permute-start.33 = (bf16[1,1024]{1,0:T(2,128)(2,1)S(1)}, bf16[1,1024]{1,0:T(2,128)(2,1)S(1)}, u32[]{:S(2)}, u32[]{:S(2)}) collective-permute-start(bf16[1,1024]{1,0:T(2,128)(2,1)S(1)} %reshape.2714), channel_id=1, source_target_pairs={{0,3},{1,4},{2,5},{3,6},{4,7},{5,8},{6,9},{7,10},{8,11},{9,12},{10... | collective-permute-start | bytes 6152 | tf_op jit(solution)/shard_map/ppermute | solution.py:14
  180.5 57.6 %copy-start.3 = (bf16[16,4096]{1,0:T(8,128)(2,1)}, bf16[16,4096]{1,0:T(8,128)(2,1)S(1)}, u32[]{:S(2)}) copy-start(bf16[16,4096]{1,0:T(8,128)(2,1)S(1)} %add_convert_fusion.1) | copy-start | bytes 393220
  180.6 57.6 %copy-start.42 = (s32[512]{0:T(512)S(1)}, s32[512]{0:T(512)}, u32[]{:S(2)}) copy-start(s32[512]{0:T(512)} %copy-done.41) | copy-start | bytes 6148
  180.8 100.5 %collective-permute-start.26 = (bf16[30,1024]{1,0:T(8,128)(2,1)S(1)}, bf16[30,1024]{1,0:T(8,128)(2,1)S(1)}, u32[]{:S(2)}, u32[]{:S(2)}) collective-permute-start(bf16[30,1024]{1,0:T(8,128)(2,1)S(1)} %reshape.2707), channel_id=1, source_target_pairs={{1,0},{2,1},{3,2},{4,3},{5,4},{6,5},{7,6},{8,7},{9,8},{10,9},{11,1... | collective-permute-start | bytes 184328 | tf_op jit(solution)/shard_map/ppermute | solution.py:14
  182.5 12.1 %collective-permute-start.39 = (bf16[1,1024]{1,0:T(2,128)(2,1)S(1)}, bf16[1,1024]{1,0:T(2,128)(2,1)S(1)}, u32[]{:S(2)}, u32[]{:S(2)}) collective-permute-start(bf16[1,1024]{1,0:T(2,128)(2,1)S(1)} %reshape.2718), channel_id=1, source_target_pairs={{2,0},{3,1},{4,2},{5,3},{6,4},{7,5},{8,6},{9,7},{10,8},{11,9},{12,... | collective-permute-start | bytes 6152 | tf_op jit(solution)/shard_map/ppermute | solution.py:14
  183.8 16.9 %collective-permute-start.35 = (bf16[1,1024]{1,0:T(2,128)(2,1)S(1)}, bf16[1,1024]{1,0:T(2,128)(2,1)S(1)}, u32[]{:S(2)}, u32[]{:S(2)}) collective-permute-start(bf16[1,1024]{1,0:T(2,128)(2,1)S(1)} %reshape.2718), channel_id=1, source_target_pairs={{6,0},{7,1},{8,2},{9,3},{10,4},{11,5},{12,6},{13,7},{14,8},{15,9},... | collective-permute-start | bytes 6152 | tf_op jit(solution)/shard_map/ppermute | solution.py:14
  185.1 16.9 %collective-permute-start.36 = (bf16[1,1024]{1,0:T(2,128)(2,1)S(1)}, bf16[1,1024]{1,0:T(2,128)(2,1)S(1)}, u32[]{:S(2)}, u32[]{:S(2)}) collective-permute-start(bf16[1,1024]{1,0:T(2,128)(2,1)S(1)} %reshape.2718), channel_id=1, source_target_pairs={{4,0},{5,1},{6,2},{7,3},{8,4},{9,5},{10,6},{11,7},{12,8},{13,9},{1... | collective-permute-start | bytes 6152 | tf_op jit(solution)/shard_map/ppermute | solution.py:14
  186.4 16.9 %collective-permute-start.37 = (bf16[1,1024]{1,0:T(2,128)(2,1)S(1)}, bf16[1,1024]{1,0:T(2,128)(2,1)S(1)}, u32[]{:S(2)}, u32[]{:S(2)}) collective-permute-start(bf16[1,1024]{1,0:T(2,128)(2,1)S(1)} %reshape.2718), channel_id=1, source_target_pairs={{0,4},{1,5},{2,6},{3,7},{4,8},{5,9},{6,10},{7,11},{8,12},{9,13},{1... | collective-permute-start | bytes 6152 | tf_op jit(solution)/shard_map/ppermute | solution.py:14
  194.6 14.2 %collective-permute-start.38 = (bf16[1,1024]{1,0:T(2,128)(2,1)S(1)}, bf16[1,1024]{1,0:T(2,128)(2,1)S(1)}, u32[]{:S(2)}, u32[]{:S(2)}) collective-permute-start(bf16[1,1024]{1,0:T(2,128)(2,1)S(1)} %reshape.2718), channel_id=1, source_target_pairs={{0,6},{1,7},{2,8},{3,9},{4,10},{5,11},{6,12},{7,13},{8,14},{9,15},... | collective-permute-start | bytes 6152 | tf_op jit(solution)/shard_map/ppermute | solution.py:14
  200.7 10.7 %collective-permute-start.40 = (bf16[1,1024]{1,0:T(2,128)(2,1)S(1)}, bf16[1,1024]{1,0:T(2,128)(2,1)S(1)}, u32[]{:S(2)}, u32[]{:S(2)}) collective-permute-start(bf16[1,1024]{1,0:T(2,128)(2,1)S(1)} %reshape.2722), channel_id=1, source_target_pairs={{12,0},{13,1},{14,2},{15,3},{28,16},{29,17},{30,18},{31,19}} | collective-permute-start | bytes 6152 | tf_op jit(solution)/shard_map/ppermute | solution.py:14
  202.0 10.7 %collective-permute-start.41 = (bf16[1,1024]{1,0:T(2,128)(2,1)S(1)}, bf16[1,1024]{1,0:T(2,128)(2,1)S(1)}, u32[]{:S(2)}, u32[]{:S(2)}) collective-permute-start(bf16[1,1024]{1,0:T(2,128)(2,1)S(1)} %reshape.2722), channel_id=1, source_target_pairs={{8,0},{9,1},{10,2},{11,3},{12,4},{13,5},{14,6},{15,7},{24,16},{25,... | collective-permute-start | bytes 6152 | tf_op jit(solution)/shard_map/ppermute | solution.py:14
  203.3 10.7 %collective-permute-start.42 = (bf16[1,1024]{1,0:T(2,128)(2,1)S(1)}, bf16[1,1024]{1,0:T(2,128)(2,1)S(1)}, u32[]{:S(2)}, u32[]{:S(2)}) collective-permute-start(bf16[1,1024]{1,0:T(2,128)(2,1)S(1)} %reshape.2722), channel_id=1, source_target_pairs={{0,8},{1,9},{2,10},{3,11},{4,12},{5,13},{6,14},{7,15},{16,24},{17,... | collective-permute-start | bytes 6152 | tf_op jit(solution)/shard_map/ppermute | solution.py:14
  208.8 10.5 %collective-permute-start.43 = (bf16[1,1024]{1,0:T(2,128)(2,1)S(1)}, bf16[1,1024]{1,0:T(2,128)(2,1)S(1)}, u32[]{:S(2)}, u32[]{:S(2)}) collective-permute-start(bf16[1,1024]{1,0:T(2,128)(2,1)S(1)} %reshape.2722), channel_id=1, source_target_pairs={{0,12},{1,13},{2,14},{3,15},{16,28},{17,29},{18,30},{19,31}} | collective-permute-start | bytes 6152 | tf_op jit(solution)/shard_map/ppermute | solution.py:14
  211.4 70.0 %collective-permute-start.28 = (bf16[30,1024]{1,0:T(8,128)(2,1)S(1)}, bf16[30,1024]{1,0:T(8,128)(2,1)S(1)}, u32[]{:S(2)}, u32[]{:S(2)}) collective-permute-start(bf16[30,1024]{1,0:T(8,128)(2,1)S(1)} %reshape.2707), channel_id=1, source_target_pairs={{2,0},{3,1},{4,2},{5,3},{6,4},{7,5},{8,6},{9,7},{10,8},{11,9},{12,... | collective-permute-start | bytes 184328 | tf_op jit(solution)/shard_map/ppermute | solution.py:14
  212.7 68.8 %collective-permute-start.27 = (bf16[30,1024]{1,0:T(8,128)(2,1)S(1)}, bf16[30,1024]{1,0:T(8,128)(2,1)S(1)}, u32[]{:S(2)}, u32[]{:S(2)}) collective-permute-start(bf16[30,1024]{1,0:T(8,128)(2,1)S(1)} %reshape.2707), channel_id=1, source_target_pairs={{0,1},{1,2},{2,3},{3,4},{4,5},{5,6},{6,7},{7,8},{8,9},{9,10},{10,1... | collective-permute-start | bytes 184328 | tf_op jit(solution)/shard_map/ppermute | solution.py:14
  214.0 16.4 %collective-permute-start.24 = (bf16[16,768]{1,0:T(8,128)(2,1)S(1)}, bf16[16,768]{1,0:T(8,128)(2,1)S(1)}, u32[]{:S(2)}, u32[]{:S(2)}) collective-permute-start(bf16[16,768]{1,0:T(8,128)(2,1)S(1)} %get-tuple-element.291), channel_id=1, source_target_pairs={{0,1},{1,2},{2,3},{3,4},{4,5},{5,6},{6,7},{7,8},{8,9},{9,10},{10,1... | collective-permute-start | bytes 73736 | tf_op jit(solution)/shard_map/ppermute | solution.py:24
  220.2 5.9 %collective-permute-start.44 = (bf16[1,1024]{1,0:T(2,128)(2,1)S(1)}, bf16[1,1024]{1,0:T(2,128)(2,1)S(1)}, u32[]{:S(2)}, u32[]{:S(2)}) collective-permute-start(bf16[1,1024]{1,0:T(2,128)(2,1)S(1)} %reshape.2724), channel_id=1, source_target_pairs={{0,2},{1,3},{2,4},{3,5},{4,6},{5,7},{6,8},{7,9},{8,10},{9,11},{10,... | collective-permute-start | bytes 6152 | tf_op jit(solution)/shard_map/ppermute | solution.py:14
  226.6 2.1 collective-permute-start.45
  228.7 9.4 %collective-permute-start.25 = (bf16[16,768]{1,0:T(8,128)(2,1)S(1)}, bf16[16,768]{1,0:T(8,128)(2,1)S(1)}, u32[]{:S(2)}, u32[]{:S(2)}) collective-permute-start(bf16[16,768]{1,0:T(8,128)(2,1)S(1)} %get-tuple-element.292), channel_id=1, source_target_pairs={{1,0},{2,1},{3,2},{4,3},{5,4},{6,5},{7,6},{8,7},{9,8},{10,9},{11,1... | collective-permute-start | bytes 73736 | tf_op jit(solution)/shard_map/ppermute | solution.py:25
  230.4 51.2 %collective-permute-start.29 = (bf16[30,1024]{1,0:T(8,128)(2,1)S(1)}, bf16[30,1024]{1,0:T(8,128)(2,1)S(1)}, u32[]{:S(2)}, u32[]{:S(2)}) collective-permute-start(bf16[30,1024]{1,0:T(8,128)(2,1)S(1)} %reshape.2707), channel_id=1, source_target_pairs={{0,2},{1,3},{2,4},{3,5},{4,6},{5,7},{6,8},{7,9},{8,10},{9,11},{10,... | collective-permute-start | bytes 184328 | tf_op jit(solution)/shard_map/ppermute | solution.py:14
  238.2 43.5 %copy-start.18 = (pred[2]{0:T(512)(128)(4,1)S(1)}, pred[2]{0:T(512)(128)(4,1)}, u32[]{:S(2)}) copy-start(pred[2]{0:T(512)(128)(4,1)} %get-tuple-element.330) | copy-start | bytes 10
  238.2 43.5 %copy-start.20 = (pred[2]{0:T(512)(128)(4,1)S(1)}, pred[2]{0:T(512)(128)(4,1)}, u32[]{:S(2)}) copy-start(pred[2]{0:T(512)(128)(4,1)} %get-tuple-element.331) | copy-start | bytes 10
  238.2 43.5 %copy-start.22 = (pred[2]{0:T(512)(128)(4,1)S(1)}, pred[2]{0:T(512)(128)(4,1)}, u32[]{:S(2)}) copy-start(pred[2]{0:T(512)(128)(4,1)} %get-tuple-element.332) | copy-start | bytes 10
  238.2 43.5 %copy-start.24 = (pred[2]{0:T(512)(128)(4,1)S(1)}, pred[2]{0:T(512)(128)(4,1)}, u32[]{:S(2)}) copy-start(pred[2]{0:T(512)(128)(4,1)} %get-tuple-element.333) | copy-start | bytes 10
  238.2 43.5 %copy-start.26 = (pred[2]{0:T(512)(128)(4,1)S(1)}, pred[2]{0:T(512)(128)(4,1)}, u32[]{:S(2)}) copy-start(pred[2]{0:T(512)(128)(4,1)} %get-tuple-element.337) | copy-start | bytes 10
  238.2 43.5 %copy-start.28 = (pred[2]{0:T(512)(128)(4,1)S(1)}, pred[2]{0:T(512)(128)(4,1)}, u32[]{:S(2)}) copy-start(pred[2]{0:T(512)(128)(4,1)} %get-tuple-element.338) | copy-start | bytes 10
  238.3 43.6 %copy-start.10 = (pred[2]{0:T(512)(128)(4,1)S(1)}, pred[2]{0:T(512)(128)(4,1)}, u32[]{:S(2)}) copy-start(pred[2]{0:T(512)(128)(4,1)} %copy-done.9) | copy-start | bytes 10
  238.3 43.6 %copy-start.12 = (pred[2]{0:T(512)(128)(4,1)S(1)}, pred[2]{0:T(512)(128)(4,1)}, u32[]{:S(2)}) copy-start(pred[2]{0:T(512)(128)(4,1)} %copy-done.11) | copy-start | bytes 10
  238.3 43.6 %copy-start.14 = (pred[2]{0:T(512)(128)(4,1)S(1)}, pred[2]{0:T(512)(128)(4,1)}, u32[]{:S(2)}) copy-start(pred[2]{0:T(512)(128)(4,1)} %copy-done.13) | copy-start | bytes 10
  238.3 43.6 %copy-start.16 = (pred[2]{0:T(512)(128)(4,1)S(1)}, pred[2]{0:T(512)(128)(4,1)}, u32[]{:S(2)}) copy-start(pred[2]{0:T(512)(128)(4,1)} %copy-done.15) | copy-start | bytes 10
  (26 other events, 253.1 us)
where the time goes:
time: 289 us; the launch traced here: 287 us
  starting transfers between devices  136 us (47%)
  matrix products  70.8 us (24%)
  between operations  32.9 us (11%)
  local copies, waits for them, and re-layouts  26.8 us (9%)
  loops' own time  10.7 us (4%)
  other arithmetic  5.66 us (2%)
  waiting for transfers between devices  3.96 us (1%)
    ppermute x40, starting transfers between devices, from_behind(): lax.ppermute(value, axis, [(source, source + steps) for source in range(l...  119 us
    dot_general x16, matrix products, one_block(): lax.dot_general(inputs, weights, (((1,), (1,)), ((), ())), preferred_elem...  62.8 us
    ppermute x3, starting transfers between devices, extended_2(): before = lax.ppermute(last, axis, up)  13.6 us
    another operation x2, loops' own time, near_field(): blocks = lax.map(one_block, jnp.arange(leaf_count // 2, dtype=jnp.int32))  10.7 us
    dynamic_slice x16, local copies, waits for them, and re-layouts, near_field(): blocks = lax.map(one_block, jnp.arange(leaf_count // 2, dtype=jnp.int32))  9.46 us
  transfers between devices with their start and end apart: 46, of which 4 were waited for; matrix products, arithmetic and copies ran while one was open for 30% of the time, Pallas kernels for 0%

commit v1 on v0

v1 whole, which is shorter than its diff:
```python
import functools

import jax
import jax.numpy as jnp
from jax import lax
from jax.experimental import pallas as pl
from jax.experimental.pallas import tpu as pltpu
from jax.sharding import PartitionSpec as P

AXES = ("leaf", "sub", "rep")
MESH = pl.DeviceIdType.MESH
F32 = jnp.float32
BF16 = jnp.bfloat16
I32 = jnp.int32
AMPLITUDE = 0.15
SLOPE = 1.7320508075688772 / 0.3
LOG2E = 1.4426950408889634
GAIN = SLOPE * LOG2E
LINEAR = AMPLITUDE / LOG2E
REACH = 3
HALO = 2
PAD = 3
FEATS = 32
UNROLL = 16


def repeat(count, step):
    if count <= UNROLL:
        for index in range(count):
            step(index)
    else:

        def once(index, carry):
            step(index)
            return carry

        lax.fori_loop(0, count, once, 0)


def dot(a, b):
    return lax.dot_general(a, b, (((1,), (0,)), ((), ())), preferred_element_type=F32)


def dot_t(a, b):
    return lax.dot_general(a, b, (((1,), (1,)), ((), ())), preferred_element_type=F32)


def twice(c):
    return jnp.concatenate([c, c], axis=1).astype(BF16)


def pieces(x):
    high = x.astype(BF16).astype(F32)
    rest = x - high
    mid = rest.astype(BF16).astype(F32)
    return high, mid, rest - mid


def kernel(
    sizes,
    vectors,
    positions,
    bases,
    low_pairs,
    low_tiles,
    low_lists,
    top_pairs,
    top_tiles,
    top_lists,
    first,
    second,
    weights,
    vx,
    nacc,
    feat_a,
    feat_b,
    tgt,
    src,
    pos_send,
    pos_recv,
    cx,
    c_send,
    c_recv,
    terms,
    low_exp,
    top_exp,
    own_exp,
    tiles_held,
    top_coeffs,
    upper_coeffs,
    pairs_held,
    sems,
):
    leaf_size, sub_size, rep_size = sizes
    shards = leaf_size * sub_size * rep_size
    leaves, rank, pts = bases.shape
    columns = vectors.shape[0]
    length = leaves * pts
    wing = REACH * pts
    levels = leaves.bit_length() - 1
    amounts = [leaves >> h for h in range(levels)]
    starts = [sum(amounts[:h]) for h in range(levels)]
    pair_starts = [sum(amounts[1 : h + 1]) for h in range(levels)]
    c_starts = [sum(amounts[:h]) + 2 * HALO * h for h in range(levels)]
    top_count = top_tiles.shape[1]
    top_edges = top_count - 1
    me = (lax.axis_index("leaf") * sub_size + lax.axis_index("sub")) * rep_size + lax.axis_index(
        "rep"
    )

    def place(s):
        return {
            "leaf": s // (sub_size * rep_size),
            "sub": (s // rep_size) % sub_size,
            "rep": s % rep_size,
        }

    names = iter(range(1000))

    def pair_of_sems():
        return sems.at[next(names)], sems.at[next(names)]

    def remote(source, dest, both, peer):
        return pltpu.make_async_remote_copy(
            src_ref=source,
            dst_ref=dest,
            send_sem=both[0],
            recv_sem=both[1],
            device_id=place(peer),
            device_id_type=MESH,
        )

    has_left = me > 0
    has_right = me < shards - 1

    class Exchange:
        def __init__(self, to_right, from_left, to_left, from_right):
            self.up = remote(to_right, from_left, pair_of_sems(), jnp.minimum(me + 1, shards - 1))
            self.down = remote(to_left, from_right, pair_of_sems(), jnp.maximum(me - 1, 0))

        def start(self):
            pl.when(has_right)(self.up.start)
            pl.when(has_left)(self.down.start)

        def arrive(self):
            pl.when(has_left)(self.up.wait_recv)
            pl.when(has_right)(self.down.wait_recv)

        def sent(self):
            pl.when(has_right)(self.up.wait_send)
            pl.when(has_left)(self.down.wait_send)

    barrier = pltpu.get_barrier_semaphore()

    def greet(k):
        pl.semaphore_signal(
            barrier, inc=1, device_id=place((me + k + 1) % shards), device_id_type=MESH
        )

    repeat(shards - 1, greet)

    lane = lax.broadcasted_iota(I32, (columns, 2 * rank), 1)
    is_left = lane < rank

    def expand(lists):
        block = lax.broadcasted_iota(I32, (lists.shape[0], 4 * rank), 1) // rank
        out = jnp.broadcast_to(lists[:, 3:4], block.shape)
        for k in range(3):
            out = jnp.where(block == k, jnp.broadcast_to(lists[:, k : k + 1], block.shape), out)
        return out

    low_exp[...] = expand(low_lists[...])
    wide = expand(top_lists[0])
    for t in range(top_count):
        own_exp[t] = jnp.broadcast_to(wide[t : t + 1], (8, 4 * rank))

    zeros_pad = jnp.zeros((PAD, columns, 2 * rank), BF16)
    for p in range(2):
        top_coeffs[p, 0:PAD] = zeros_pad
        top_coeffs[p, PAD + shards : PAD + shards + PAD] = zeros_pad
    for t in range(top_edges):
        count = shards >> (t + 1)
        upper_coeffs[t, 0:PAD] = zeros_pad
        upper_coeffs[t, PAD + count : PAD + count + PAD] = zeros_pad

    @pl.when(me == 0)
    def _():
        pos_recv[0] = jnp.zeros(pos_recv.shape[1:], F32)
        for p in range(2):
            vx[p, :, 0:wing] = jnp.zeros((columns, wing), BF16)
            c_recv[p, 0] = jnp.zeros(c_recv.shape[2:], BF16)

    @pl.when(me == shards - 1)
    def _():
        pos_recv[1] = jnp.zeros(pos_recv.shape[1:], F32)
        for p in range(2):
            vx[p, :, wing + length :] = jnp.zeros((columns, wing), BF16)
            c_recv[p, 1] = jnp.zeros(c_recv.shape[2:], BF16)

    pos_send[...] = jnp.zeros(pos_send.shape, F32)
    pos_send[0, 0:3, :] = positions[:, 0:wing]
    pos_send[1, 0:3, :] = positions[:, length - wing :]
    vx[0, :, wing : wing + length] = vectors[...]

    pl.semaphore_wait(barrier, shards - 1)

    pos_move = Exchange(pos_send.at[1], pos_recv.at[0], pos_send.at[0], pos_recv.at[1])
    pos_move.start()
    v_moves = [
        Exchange(
            vx.at[p, :, length : wing + length],
            vx.at[p, :, 0:wing],
            vx.at[p, :, wing : 2 * wing],
            vx.at[p, :, wing + length : 2 * wing + length],
        )
        for p in range(2)
    ]
    v_moves[0].start()

    tile_sems = [pair_of_sems() for t in range(top_count)]
    list_sems = [pair_of_sems() for t in range(top_count)]
    edge_sems = [pair_of_sems() for t in range(top_edges)]

    def send_tops():
        tiles_held[0] = top_tiles[0, 0]
        top_exp[0] = own_exp[0]
        for t in range(1, top_count):

            @pl.when(me % (1 << t) == 0)
            def _(t=t):
                tiles_held[t] = top_tiles[0, t]
                top_exp[t] = own_exp[t]

                def push(k):
                    remote(top_tiles.at[0, t], tiles_held.at[t], tile_sems[t], me + k + 1).start()
                    remote(own_exp.at[t], top_exp.at[t], list_sems[t], me + k + 1).start()

                repeat((1 << t) - 1, push)

        for t in range(top_edges):

            @pl.when(me % (2 << t) == 0)
            def _(t=t):
                slot = me // (2 << t)
                pairs_held[t, slot] = top_pairs[0, t]

                def push(k):
                    remote(
                        top_pairs.at[0, t],
                        pairs_held.at[t, slot],
                        edge_sems[t],
                        (me + k + 1) % shards,
                    ).start()

                repeat(shards - 1, push)

    def wait_bytes(ref, sem):
        pltpu.make_async_copy(ref, ref, sem).wait()

    def arrive_tops():
        for t in range(1, top_count):

            @pl.when(me % (1 << t) != 0)
            def _(t=t):
                wait_bytes(tiles_held.at[t], tile_sems[t][1])
                wait_bytes(top_exp.at[t], list_sems[t][1])

        for t in range(top_edges):
            count = shards >> (t + 1)

            @pl.when(me % (2 << t) == 0)
            def _(t=t, count=count):
                wait_bytes(pairs_held.at[t, 0 : count - 1], edge_sems[t][1])

            @pl.when(me % (2 << t) != 0)
            def _(t=t, count=count):
                wait_bytes(pairs_held.at[t, 0:count], edge_sems[t][1])

    def sent_tops():
        for t in range(1, top_count):

            @pl.when(me % (1 << t) == 0)
            def _(t=t):
                def one(k):
                    wait_bytes(tiles_held.at[t], tile_sems[t][0])
                    wait_bytes(top_exp.at[t], list_sems[t][0])

                repeat((1 << t) - 1, one)

        for t in range(top_edges):

            @pl.when(me % (2 << t) == 0)
            def _(t=t):
                def one(k):
                    wait_bytes(pairs_held.at[t, 0], edge_sems[t][0])

                repeat(shards - 1, one)

    c_moves = [
        Exchange(c_send.at[p, 1], c_recv.at[p, 0], c_send.at[p, 0], c_recv.at[p, 1])
        for p in range(2)
    ]
    root_sems = [pair_of_sems() for p in range(2)]

    def rows(h, j):
        begin = (c_starts[h] + HALO + j) * columns
        return slice(begin, begin + columns)

    def joined_of(left, right):
        return jnp.where(is_left, left.astype(F32), right.astype(F32)).astype(BF16)

    def upsweep(p):
        for leaf in range(leaves):
            begin = wing + leaf * pts
            cx[rows(0, leaf), :] = twice(dot_t(vx[p, :, begin : begin + pts], bases[leaf]))
        for h in range(levels):
            for i in range(amounts[h] // 2):
                joined = joined_of(cx[rows(h, 2 * i), :], cx[rows(h, 2 * i + 1), :])
                c = twice(dot_t(joined, low_pairs[pair_starts[h] + i]))
                if h + 1 < levels:
                    cx[rows(h + 1, i), :] = c
                else:
                    top_coeffs[p, PAD + me] = c

        def push(k):
            slot = top_coeffs.at[p, PAD + me]
            remote(slot, slot, root_sems[p], (me + k + 1) % shards).start()

        repeat(shards - 1, push)
        for h in range(levels):
            n = amounts[h]
            for j in range(HALO):
                at = slice((HALO * h + j) * columns, (HALO * h + j + 1) * columns)
                c_send[p, 0, at, :] = cx[rows(h, j), :]
                c_send[p, 1, at, :] = cx[rows(h, n - HALO + j), :]
        c_moves[p].start()

    def near(p, leaf):
        at = leaf + REACH
        total = dot(vx[p, :, at * pts : (at + REACH + 1) * pts], weights[at])
        for d in range(1, REACH + 1):
            begin = (at - d) * pts
            total = total + dot_t(
                vx[p, :, begin : begin + pts], weights[at - d, d * pts : (d + 1) * pts, :]
            )
        nacc[:, leaf * pts : (leaf + 1) * pts] = total

    def couple(row, before, after, far, far_offset, tile):
        before, after, far = (x.astype(F32) for x in (before, after, far))
        none = jnp.zeros_like(before)
        halves = []
        for half in range(2):
            listed = jnp.broadcast_to(row[:, half * 2 * rank : (half + 1) * 2 * rank], none.shape)
            value = jnp.where(listed == far_offset, far, none)
            value = jnp.where(listed == 2, after, value)
            value = jnp.where(listed == -2, before, value)
            halves.append(value.astype(BF16))
        return dot_t(jnp.concatenate(halves, axis=1), tile)

    def finish(p, out):
        c_moves[p].arrive()
        for h in range(levels):
            n = amounts[h]
            for j in range(HALO):
                at = slice((HALO * h + j) * columns, (HALO * h + j + 1) * columns)
                cx[rows(h, j - HALO), :] = c_recv[p, 0, at, :]
                cx[rows(h, n + j), :] = c_recv[p, 1, at, :]
        for h in range(levels):
            for i in range(amounts[h]):
                offset = -3 if i % 2 else 3
                index = starts[h] + i
                terms[index * columns : (index + 1) * columns, :] = couple(
                    low_exp[index : index + 1, :],
                    cx[rows(h, i - 2), :],
                    cx[rows(h, i + 2), :],
                    cx[rows(h, i + offset), :],
                    offset,
                    low_tiles[index],
                )

        if p == 0:
            arrive_tops()
        wait_bytes(top_coeffs.at[p, 0 : shards - 1], root_sems[p][1])

        def held(t):
            return top_coeffs.at[p] if t == 0 else upper_coeffs.at[t - 1]

        for t in range(top_edges):
            lower_level = held(t)
            upper_level = held(t + 1)

            def lift(i, t=t, lower_level=lower_level, upper_level=upper_level):
                joined = joined_of(lower_level[PAD + 2 * i], lower_level[PAD + 2 * i + 1])
                upper_level[PAD + i] = twice(dot_t(joined, pairs_held[t, i]))

            repeat(shards >> (t + 1), lift)

        field = None
        for t in range(top_count - 1, -1, -1):
            index = me // (1 << t)
            odd = index % 2
            offset = 3 - 6 * odd
            level = held(t)
            term = couple(
                top_exp[t, 0:1, :],
                level[PAD + index - 2],
                level[PAD + index + 2],
                level[PAD + index + offset],
                offset,
                tiles_held[t],
            )
            if field is not None:
                spread = dot(field, pairs_held[t, index // 2])
                share = jnp.where(
                    jnp.full((columns, rank), odd, I32) == 0, spread[:, :rank], spread[:, rank:]
                )
                term = term + share.astype(BF16).astype(F32)
            field = term.astype(BF16)

        fields = [field]
        for h in range(levels - 1, -1, -1):
            below = []
            for i in range(amounts[h]):
                if i % 2 == 0:
                    spread = dot(fields[i // 2], low_pairs[pair_starts[h] + i // 2])
                    spread = spread.astype(BF16).astype(F32)
                    share = spread[:, :rank]
                else:
                    share = spread[:, rank:]
                index = starts[h] + i
                below.append(
                    (terms[index * columns : (index + 1) * columns, :] + share).astype(BF16)
                )
            fields = below
        for leaf in range(leaves):
            at = slice(leaf * pts, (leaf + 1) * pts)
            value = (nacc[:, at] + dot(fields[leaf], bases[leaf])).astype(BF16)
            out[:, at] = value
            if p == 0:
                vx[1, :, wing + leaf * pts : wing + (leaf + 1) * pts] = value

    shift = jnp.where(
        lax.broadcasted_iota(I32, (3, pts), 0) == 0,
        (me * leaves).astype(F32) * 0.25,
        jnp.zeros((3, pts), F32),
    )
    feat_a[...] = jnp.zeros(feat_a.shape, F32)
    feat_b[...] = jnp.zeros(feat_b.shape, F32)
    feat_a[21:24, :] = jnp.ones((3, pts), F32)
    feat_b[18:21, :] = jnp.ones((3, pts), F32)

    def features(position, leaf):
        x = (position - shift) * GAIN
        high, mid, low = pieces(x)
        square = x * x
        norms = pieces(square[0:1] + square[1:2] + square[2:3])
        for k, part in enumerate((high, mid, high, mid, low, high)):
            feat_a[3 * k : 3 * k + 3, :] = part
        for k, part in enumerate((high, high, mid, mid, high, low)):
            feat_b[3 * k : 3 * k + 3, :] = -2.0 * part
        for k in range(3):
            feat_a[18 + k : 19 + k, :] = norms[k]
            feat_b[21 + k : 22 + k, :] = norms[k]
        at = slice(leaf * pts, (leaf + 1) * pts)
        tgt[:, at] = feat_a[...].astype(BF16)
        src[at, :] = jnp.transpose(feat_b[...]).astype(BF16)

    def evaluate(a):
        right = tgt[:, pl.ds(pl.multiple_of(a * pts, pts), pts)]
        for b in range(REACH + 1):
            left = src[pl.ds(pl.multiple_of((a + b) * pts, pts), pts), :]
            square = jnp.maximum(dot(left, right), 1e-30)
            u = square * lax.rsqrt(square)
            value = (AMPLITUDE + LINEAR * u) * jnp.exp2(-u)
            weights[a, b * pts : (b + 1) * pts, :] = value.astype(BF16)

    def evaluate_from(begin, end):
        def once(a, carry):
            evaluate(a)
            return carry

        lax.fori_loop(begin, end, once, 0)

    send_tops()
    upsweep(0)
    for leaf in range(leaves):
        features(positions[:, leaf * pts : (leaf + 1) * pts], leaf + REACH)
    evaluate_from(REACH, leaves)
    pos_move.arrive()
    for k in range(REACH):
        features(pos_recv[0, 0:3, k * pts : (k + 1) * pts], k)
        features(pos_recv[1, 0:3, k * pts : (k + 1) * pts], REACH + leaves + k)
    evaluate_from(0, REACH)
    evaluate_from(leaves, leaves + REACH)
    v_moves[0].arrive()
    for leaf in range(leaves):
        near(0, leaf)
    finish(0, first)

    v_moves[1].start()
    upsweep(1)
    for leaf in range(REACH, leaves - REACH):
        near(1, leaf)
    v_moves[1].arrive()
    for leaf in list(range(REACH)) + list(range(leaves - REACH, leaves)):
        near(1, leaf)
    finish(1, second)

    pos_move.sent()
    sent_tops()
    for p in range(2):
        v_moves[p].sent()
        c_moves[p].sent()
        wait_bytes(top_coeffs.at[p, 0 : shards - 1], root_sems[p][0])


def body(sizes, *args):
    vectors, positions, bases, low_pairs, low_tiles, low_lists, top_pairs, top_tiles, top_lists = (
        args
    )
    columns, length = vectors.shape
    leaves, rank, pts = bases.shape
    shards = sizes[0] * sizes[1] * sizes[2]
    levels = leaves.bit_length() - 1
    clusters = low_tiles.shape[0]
    top_count = top_tiles.shape[1]
    spread = leaves + 2 * REACH
    wing = REACH * pts
    vmem = pl.BlockSpec(memory_space=pltpu.VMEM)
    out = jax.ShapeDtypeStruct((columns, length), BF16)
    return pl.pallas_call(
        functools.partial(kernel, sizes),
        out_shape=(out, out),
        in_specs=[vmem] * 9,
        out_specs=(vmem, vmem),
        scratch_shapes=[
            pltpu.VMEM((leaves + REACH, (REACH + 1) * pts, pts), BF16),
            pltpu.VMEM((2, columns, spread * pts), BF16),
            pltpu.VMEM((columns, length), F32),
            pltpu.VMEM((FEATS, pts), F32),
            pltpu.VMEM((FEATS, pts), F32),
            pltpu.VMEM((FEATS, spread * pts), BF16),
            pltpu.VMEM((spread * pts, FEATS), BF16),
            pltpu.VMEM((2, 8, wing), F32),
            pltpu.VMEM((2, 8, wing), F32),
            pltpu.VMEM(((clusters + 2 * HALO * levels) * columns, 2 * rank), BF16),
            pltpu.VMEM((2, 2, HALO * levels * columns, 2 * rank), BF16),
            pltpu.VMEM((2, 2, HALO * levels * columns, 2 * rank), BF16),
            pltpu.VMEM((clusters * columns, rank), F32),
            pltpu.VMEM((clusters, 4 * rank), I32),
            pltpu.VMEM((top_count, 8, 4 * rank), I32),
            pltpu.VMEM((top_count, 8, 4 * rank), I32),
            pltpu.VMEM((top_count, rank, 4 * rank), BF16),
            pltpu.VMEM((2, shards + 2 * PAD, columns, 2 * rank), BF16),
            pltpu.VMEM(
                (top_count - 1, shards // 2 + 2 * PAD, columns, 2 * rank), BF16
            ),
            pltpu.VMEM((top_count - 1, shards // 2, rank, 2 * rank), BF16),
            pltpu.SemaphoreType.DMA((64,)),
        ],
        compiler_params=pltpu.CompilerParams(
            collective_id=0, has_side_effects=True, vmem_limit_bytes=48 * 1024 * 1024
        ),
    )(*args)


def solution(mesh):
    everywhere = ("groups",) + AXES
    placed = (
        P(None, everywhere),
        P(None, everywhere),
        P(everywhere, None, None),
        P(everywhere, None, None),
        P(everywhere, None, None),
        P(everywhere, None),
        P(everywhere, None, None, None),
        P(everywhere, None, None, None),
        P(everywhere, None, None),
    )
    sizes = tuple(mesh.shape[axis] for axis in AXES)
    return jax.shard_map(
        functools.partial(body, sizes),
        mesh=mesh,
        in_specs=placed,
        out_specs=(P(None, everywhere), P(None, everywhere)),
        check_vma=False,
    )
```

time: 289 us -> 38.4 us (0.13)
  starting transfers between devices: 136 us -> 0 us
  matrix products: 70.8 us -> 0 us
  between operations: 32.9 us -> 0.66 us
  Pallas kernels: 0 us -> 28.6 us
  local copies, waits for them, and re-layouts: 26.8 us -> 8.68 us
  loops' own time: 10.7 us -> 0 us
  other arithmetic: 5.66 us -> 0 us
  waiting for transfers between devices: 3.96 us -> 0 us
    ppermute x46 -> x0, starting transfers between devices: 136 us -> none  [the longest x40 119 us: from_behind(): lax.ppermute(value, axis, [(source, source + steps) for source in range(l...]
    dot_general x44 -> x0, matrix products: 70.8 us -> none  [the longest x16 62.8 us: one_block(): lax.dot_general(inputs, weights, (((1,), (1,)), ((), ())), preferred_elem...]
    pallas_call x0 -> x1, Pallas kernels: none -> 28.6 us  [body(): pl.pallas_call(functools.partial(kernel, sizes), out_shape=(out, out), in...]
    another operation x2 -> x0, loops' own time: 10.7 us -> none  [near_field(): blocks = lax.map(one_block, jnp.arange(leaf_count // 2, dtype=jnp.int32))]
    dynamic_slice x16 -> x0, local copies, waits for them, and re-layouts: 9.46 us -> none  [near_field(): blocks = lax.map(one_block, jnp.arange(leaf_count // 2, dtype=jnp.int32))]
    slice x81 -> x0, local copies, waits for them, and re-layouts: 7.28 us -> none  [the longest x32 2.94 us: kernel_block(): delta = targets[coord_index][:, None] - sources[coord_index][None, :]]
    unnamed x90 -> x20, local copies, waits for them, and re-layouts: 1.86 us -> 8.68 us
    ppermute x46 -> x0, waiting for transfers between devices: 3.96 us -> none  [the longest x40 3.94 us: from_behind(): lax.ppermute(value, axis, [(source, source + steps) for source in range(l...]
  transfers between devices with their start and end apart: 46 -> 0, of which waited for: 4 -> 0; matrix products, arithmetic and copies ran while one was open for 30% -> 0% of each run, Pallas kernels for 0% -> 0%
where the time goes in v1:
time: 38.4 us; the launch traced here: 38 us
  Pallas kernels  28.6 us (74%)
  local copies, waits for them, and re-layouts  8.68 us (23%)
  between operations  0.66 us (2%)
    pallas_call x1, Pallas kernels, body(): pl.pallas_call(functools.partial(kernel, sizes), out_shape=(out, out), in...  28.6 us
    unnamed x20, local copies, waits for them, and re-layouts  8.68 us

profile of v1, /device:TPU:0, one launch (start us, length us, event | category | flops | bytes accessed | tf_op | source)
XLA Modules:
  0.0 38.0 jit_solution(15413504348927423311)
XLA Ops:
  0.6 0.0 copy-start.7
  0.6 0.7 %copy.12.top_lists = s32[1,3,4]{2,1,0:T(4,128)S(1)} copy(s32[1,3,4]{2,0,1:T(1,128)} %param.17) | data formatting | bytes 96 | tf_op args[8]
  1.3 0.0 copy-done.7
  1.3 0.1 copy.11.low_lists
  1.4 0.0 copy-start
  1.4 1.2 %copy-done = bf16[30,64,256]{2,1,0:T(8,128)(2,1)S(1)} copy-done((bf16[30,64,256]{2,1,0:T(8,128)(2,1)S(1)}, bf16[30,64,256]{2,1,0:T(8,128)(2,1)}, u32[]{:S(2)}) %copy-start) | copy-done | bytes 983064
  2.6 0.0 copy-start.1
  2.6 1.0 %copy-done.1 = bf16[16,64,256]{2,1,0:T(8,128)(2,1)S(1)} copy-done((bf16[16,64,256]{2,1,0:T(8,128)(2,1)S(1)}, bf16[16,64,256]{2,1,0:T(8,128)(2,1)}, u32[]{:S(2)}) %copy-start.1) | copy-done | bytes 524312
  3.7 0.0 copy-start.2
  3.7 0.9 %copy-done.2 = bf16[15,64,128]{2,1,0:T(8,128)(2,1)S(1)} copy-done((bf16[15,64,128]{2,1,0:T(8,128)(2,1)S(1)}, bf16[15,64,128]{2,1,0:T(8,128)(2,1)}, u32[]{:S(2)}) %copy-start.2) | copy-done | bytes 245784
  4.6 0.0 copy-start.3
  4.6 0.9 %copy-done.3 = bf16[16,4096]{1,0:T(8,128)(2,1)S(1)} copy-done((bf16[16,4096]{1,0:T(8,128)(2,1)S(1)}, bf16[16,4096]{1,0:T(8,128)(2,1)}, u32[]{:S(2)}) %copy-start.3) | copy-done | bytes 131096
  5.5 0.0 copy-start.4
  5.5 0.9 %copy-done.4 = bf16[1,3,64,256]{3,2,1,0:T(8,128)(2,1)S(1)} copy-done((bf16[1,3,64,256]{3,2,1,0:T(8,128)(2,1)S(1)}, bf16[1,3,64,256]{3,2,1,0:T(8,128)(2,1)}, u32[]{:S(2)}) %copy-start.4) | copy-done | bytes 98328
  6.4 0.0 copy-start.5
  6.4 0.8 %copy-done.5 = f32[3,4096]{1,0:T(4,128)S(1)} copy-done((f32[3,4096]{1,0:T(4,128)S(1)}, f32[3,4096]{1,0:T(4,128)}, u32[]{:S(2)}) %copy-start.5) | copy-done | bytes 49176
  7.3 0.0 copy-start.6
  7.3 0.8 %copy-done.6 = bf16[1,2,64,128]{3,2,1,0:T(8,128)(2,1)S(1)} copy-done((bf16[1,2,64,128]{3,2,1,0:T(8,128)(2,1)S(1)}, bf16[1,2,64,128]{3,2,1,0:T(8,128)(2,1)}, u32[]{:S(2)}) %copy-start.6) | copy-done | bytes 32792
  8.0 28.6 %shard_map.104 = (bf16[16,4096]{1,0:T(8,128)(2,1)S(1)}, bf16[16,4096]{1,0:T(8,128)(2,1)S(1)}) custom-call(bf16[16,4096]{1,0:T(8,128)(2,1)S(1)} %copy-done.3, f32[3,4096]{1,0:T(4,128)S(1)} %copy-done.5, bf16[16,64,256]{2,1,0:T(8,128)(2,1)S(1)} %copy-done.1, bf16[15,64,128]{2,1,0:T(8,128)(2,1)S(1)} %copy-done.2, bf16[30,64,256]{2,1,0:T(8,128)(2,1)S(1)} %copy-done, ...), custom_call_target="tpu_custom_call" | custom-call | tf_op jit(solution)/shard_map/pallas_call | solution.py:531
  36.7 0.7 %copy.15 = bf16[16,4096]{1,0:T(8,128)(2,1)} copy(bf16[16,4096]{1,0:T(8,128)(2,1)S(1)} %get-tuple-element.4) | data formatting | bytes 262144
  37.3 0.7 %copy.16 = bf16[16,4096]{1,0:T(8,128)(2,1)} copy(bf16[16,4096]{1,0:T(8,128)(2,1)S(1)} %get-tuple-element.5) | data formatting | bytes 262144
Async XLA Ops:
  0.6 0.7 %copy-start.7 = (s32[30,4]{0,1:T(4,128)S(1)}, s32[30,4]{0,1:T(4,128)}, u32[]{:S(2)}) copy-start(s32[30,4]{0,1:T(4,128)} %param.14) | copy-start | bytes 1444
  1.4 1.2 %copy-start = (bf16[30,64,256]{2,1,0:T(8,128)(2,1)S(1)}, bf16[30,64,256]{2,1,0:T(8,128)(2,1)}, u32[]{:S(2)}) copy-start(bf16[30,64,256]{2,1,0:T(8,128)(2,1)} %low_tiles.1) | copy-start | bytes 2949124
  2.6 1.0 %copy-start.1 = (bf16[16,64,256]{2,1,0:T(8,128)(2,1)S(1)}, bf16[16,64,256]{2,1,0:T(8,128)(2,1)}, u32[]{:S(2)}) copy-start(bf16[16,64,256]{2,1,0:T(8,128)(2,1)} %bases.1) | copy-start | bytes 1572868
  3.7 0.9 %copy-start.2 = (bf16[15,64,128]{2,1,0:T(8,128)(2,1)S(1)}, bf16[15,64,128]{2,1,0:T(8,128)(2,1)}, u32[]{:S(2)}) copy-start(bf16[15,64,128]{2,1,0:T(8,128)(2,1)} %low_pairs.1) | copy-start | bytes 737284
  4.6 0.9 %copy-start.3 = (bf16[16,4096]{1,0:T(8,128)(2,1)S(1)}, bf16[16,4096]{1,0:T(8,128)(2,1)}, u32[]{:S(2)}) copy-start(bf16[16,4096]{1,0:T(8,128)(2,1)} %vectors.1) | copy-start | bytes 393220
  5.5 0.9 %copy-start.4 = (bf16[1,3,64,256]{3,2,1,0:T(8,128)(2,1)S(1)}, bf16[1,3,64,256]{3,2,1,0:T(8,128)(2,1)}, u32[]{:S(2)}) copy-start(bf16[1,3,64,256]{3,2,1,0:T(8,128)(2,1)} %top_tiles.1) | copy-start | bytes 294916
  6.4 0.8 %copy-start.5 = (f32[3,4096]{1,0:T(4,128)S(1)}, f32[3,4096]{1,0:T(4,128)}, u32[]{:S(2)}) copy-start(f32[3,4096]{1,0:T(4,128)} %positions.1) | copy-start | bytes 147460
  7.3 0.8 %copy-start.6 = (bf16[1,2,64,128]{3,2,1,0:T(8,128)(2,1)S(1)}, bf16[1,2,64,128]{3,2,1,0:T(8,128)(2,1)}, u32[]{:S(2)}) copy-start(bf16[1,2,64,128]{3,2,1,0:T(8,128)(2,1)} %top_pairs.1) | copy-start | bytes 98308

commit v2 on v1

--- a/solution.py
+++ b/solution.py
@@ -58,17 +58,26 @@
 
 def kernel(
     sizes,
-    vectors,
+    vectors_in,
+    positions_in,
+    bases_in,
+    low_pairs_in,
+    low_tiles_in,
+    low_lists_in,
+    top_pairs_in,
+    top_tiles_in,
+    top_lists_in,
+    first,
+    second,
     positions,
     bases,
     low_pairs,
     low_tiles,
     low_lists,
+    lists_pad,
     top_pairs,
     top_tiles,
     top_lists,
-    first,
-    second,
     weights,
     vx,
     nacc,
@@ -94,7 +103,7 @@
     leaf_size, sub_size, rep_size = sizes
     shards = leaf_size * sub_size * rep_size
     leaves, rank, pts = bases.shape
-    columns = vectors.shape[0]
+    columns = vectors_in.shape[0]
     length = leaves * pts
     wing = REACH * pts
     levels = leaves.bit_length() - 1
@@ -130,6 +139,22 @@
             device_id_type=MESH,
         )
 
+    def fetch(source, dest):
+        copy = pltpu.make_async_copy(source, dest, sems.at[next(names)])
+        copy.start()
+        return copy
+
+    fetch_vectors = fetch(vectors_in, vx.at[0, :, wing : wing + length])
+    fetch_bases = fetch(bases_in, bases)
+    fetch_positions = fetch(positions_in, positions)
+    fetch_pairs = fetch(low_pairs_in, low_pairs)
+    fetch_lists = [
+        fetch(low_lists_in, low_lists),
+        fetch(top_lists_in, top_lists),
+    ]
+    fetch_tops = [fetch(top_pairs_in, top_pairs), fetch(top_tiles_in, top_tiles)]
+    fetch_tiles = fetch(low_tiles_in, low_tiles)
+
     has_left = me > 0
     has_right = me < shards - 1
 
@@ -169,10 +194,15 @@
             out = jnp.where(block == k, jnp.broadcast_to(lists[:, k : k + 1], block.shape), out)
         return out
 
-    low_exp[...] = expand(low_lists[...])
-    wide = expand(top_lists[0])
-    for t in range(top_count):
-        own_exp[t] = jnp.broadcast_to(wide[t : t + 1], (8, 4 * rank))
+    def expand_lists():
+        for copy in fetch_lists:
+            copy.wait()
+        lists_pad[...] = jnp.zeros(lists_pad.shape, I32)
+        lists_pad[0:4, 0 : low_lists.shape[1]] = low_lists[...]
+        by_cluster = jnp.transpose(lists_pad[...])
+        low_exp[...] = expand(by_cluster[: low_exp.shape[0], 0:4])
+        for t in range(top_count):
+            own_exp[t] = jnp.broadcast_to(expand(top_lists[t]), (8, 4 * rank))
 
     zeros_pad = jnp.zeros((PAD, columns, 2 * rank), BF16)
     for p in range(2):
@@ -197,15 +227,7 @@
             vx[p, :, wing + length :] = jnp.zeros((columns, wing), BF16)
             c_recv[p, 1] = jnp.zeros(c_recv.shape[2:], BF16)
 
-    pos_send[...] = jnp.zeros(pos_send.shape, F32)
-    pos_send[0, 0:3, :] = positions[:, 0:wing]
-    pos_send[1, 0:3, :] = positions[:, length - wing :]
-    vx[0, :, wing : wing + length] = vectors[...]
-
-    pl.semaphore_wait(barrier, shards - 1)
-
     pos_move = Exchange(pos_send.at[1], pos_recv.at[0], pos_send.at[0], pos_recv.at[1])
-    pos_move.start()
     v_moves = [
         Exchange(
             vx.at[p, :, length : wing + length],
@@ -215,7 +237,6 @@
         )
         for p in range(2)
     ]
-    v_moves[0].start()
 
     tile_sems = [pair_of_sems() for t in range(top_count)]
     list_sems = [pair_of_sems() for t in range(top_count)]
@@ -322,17 +343,19 @@
                 else:
                     top_coeffs[p, PAD + me] = c
 
-        def push(k):
-            slot = top_coeffs.at[p, PAD + me]
-            remote(slot, slot, root_sems[p], (me + k + 1) % shards).start()
-
-        repeat(shards - 1, push)
         for h in range(levels):
             n = amounts[h]
             for j in range(HALO):
                 at = slice((HALO * h + j) * columns, (HALO * h + j + 1) * columns)
                 c_send[p, 0, at, :] = cx[rows(h, j), :]
                 c_send[p, 1, at, :] = cx[rows(h, n - HALO + j), :]
+
+    def send_coeffs(p):
+        def push(k):
+            slot = top_coeffs.at[p, PAD + me]
+            remote(slot, slot, root_sems[p], (me + k + 1) % shards).start()
+
+        repeat(shards - 1, push)
         c_moves[p].start()
 
     def near(p, leaf):
@@ -469,10 +492,10 @@
         right = tgt[:, pl.ds(pl.multiple_of(a * pts, pts), pts)]
         for b in range(REACH + 1):
             left = src[pl.ds(pl.multiple_of((a + b) * pts, pts), pts), :]
-            square = jnp.maximum(dot(left, right), 1e-30)
+            square = jnp.maximum(dot(left, right).astype(BF16), BF16(1e-30))
             u = square * lax.rsqrt(square)
-            value = (AMPLITUDE + LINEAR * u) * jnp.exp2(-u)
-            weights[a, b * pts : (b + 1) * pts, :] = value.astype(BF16)
+            value = (BF16(AMPLITUDE) + BF16(LINEAR) * u) * jnp.exp2(-u)
+            weights[a, b * pts : (b + 1) * pts, :] = value
 
     def evaluate_from(begin, end):
         def once(a, carry):
@@ -481,8 +504,23 @@
 
         lax.fori_loop(begin, end, once, 0)
 
+    fetch_vectors.wait()
+    fetch_bases.wait()
+    fetch_pairs.wait()
+    upsweep(0)
+    fetch_positions.wait()
+    pos_send[...] = jnp.zeros(pos_send.shape, F32)
+    pos_send[0, 0:3, :] = positions[:, 0:wing]
+    pos_send[1, 0:3, :] = positions[:, length - wing :]
+    expand_lists()
+    for copy in fetch_tops:
+        copy.wait()
+
+    pl.semaphore_wait(barrier, shards - 1)
+    pos_move.start()
+    v_moves[0].start()
+    send_coeffs(0)
     send_tops()
-    upsweep(0)
     for leaf in range(leaves):
         features(positions[:, leaf * pts : (leaf + 1) * pts], leaf + REACH)
     evaluate_from(REACH, leaves)
@@ -495,10 +533,12 @@
     v_moves[0].arrive()
     for leaf in range(leaves):
         near(0, leaf)
+    fetch_tiles.wait()
     finish(0, first)
 
     v_moves[1].start()
     upsweep(1)
+    send_coeffs(1)
     for leaf in range(REACH, leaves - REACH):
         near(1, leaf)
     v_moves[1].arrive()
@@ -526,14 +566,26 @@
     top_count = top_tiles.shape[1]
     spread = leaves + 2 * REACH
     wing = REACH * pts
+    low_lists = jnp.transpose(low_lists)
+    top_lists = jnp.transpose(top_lists, (1, 0, 2))
     vmem = pl.BlockSpec(memory_space=pltpu.VMEM)
+    hbm = pl.BlockSpec(memory_space=pltpu.HBM)
     out = jax.ShapeDtypeStruct((columns, length), BF16)
     return pl.pallas_call(
         functools.partial(kernel, sizes),
         out_shape=(out, out),
-        in_specs=[vmem] * 9,
+        in_specs=[hbm] * 9,
         out_specs=(vmem, vmem),
         scratch_shapes=[
+            pltpu.VMEM(positions.shape, F32),
+            pltpu.VMEM(bases.shape, BF16),
+            pltpu.VMEM(low_pairs.shape, BF16),
+            pltpu.VMEM(low_tiles.shape, BF16),
+            pltpu.VMEM(low_lists.shape, I32),
+            pltpu.VMEM((8, 128), I32),
+            pltpu.VMEM(top_pairs.shape, BF16),
+            pltpu.VMEM(top_tiles.shape, BF16),
+            pltpu.VMEM(top_lists.shape, I32),
             pltpu.VMEM((leaves + REACH, (REACH + 1) * pts, pts), BF16),
             pltpu.VMEM((2, columns, spread * pts), BF16),
             pltpu.VMEM((columns, length), F32),
@@ -559,9 +611,19 @@
             pltpu.SemaphoreType.DMA((64,)),
         ],
         compiler_params=pltpu.CompilerParams(
-            collective_id=0, has_side_effects=True, vmem_limit_bytes=48 * 1024 * 1024
+            collective_id=0, has_side_effects=True, vmem_limit_bytes=56 * 1024 * 1024
         ),
-    )(*args)
+    )(
+        vectors,
+        positions,
+        bases,
+        low_pairs,
+        low_tiles,
+        low_lists,
+        top_pairs,
+        top_tiles,
+        top_lists,
+    )
 
 
 def solution(mesh):

time: 38.4 us -> 31 us (0.81)
  local copies, waits for them, and re-layouts: 8.68 us -> 2.26 us
  Pallas kernels: 28.6 us -> 28 us
    unnamed x20 -> x4, local copies, waits for them, and re-layouts: 8.68 us -> 2.26 us
    pallas_call x1, Pallas kernels: 28.6 us -> 28 us  [body(): pl.pallas_call(functools.partial(kernel, sizes), out_shape=(out, out), in...]
where the time goes in v2:
time: 31 us; the launch traced here: 30.9 us
  Pallas kernels  28 us (90%)
  local copies, waits for them, and re-layouts  2.26 us (7%)
  between operations  0.65 us (2%)
    pallas_call x1, Pallas kernels, body(): pl.pallas_call(functools.partial(kernel, sizes), out_shape=(out, out), in...  28 us
    unnamed x4, local copies, waits for them, and re-layouts  2.26 us

profile of v2, /device:TPU:0, one launch (start us, length us, event | category | flops | bytes accessed | tf_op | source)
XLA Modules:
  0.0 30.9 jit_solution(2375231476551020904)
XLA Ops:
  0.6 28.0 %shard_map.104 = (bf16[16,4096]{1,0:T(8,128)(2,1)}, bf16[16,4096]{1,0:T(8,128)(2,1)}) custom-call(bf16[16,4096]{1,0:T(8,128)(2,1)} %vectors_in.1, f32[3,4096]{1,0:T(4,128)} %positions_in.1, bf16[16,64,256]{2,1,0:T(8,128)(2,1)} %bases_in.1, bf16[15,64,128]{2,1,0:T(8,128)(2,1)} %low_pairs_in.1, bf16[30,64,256]{2,1,0:T(8,128)(2,1)} %low_tiles_in.1, ...), custom_call_target="tpu_custom_call" | custom-call | tf_op jit(solution)/shard_map/pallas_call | solution.py:574
  28.6 0.0 copy-start
  28.6 1.6 %copy.13 = bf16[16,4096]{1,0:T(8,128)(2,1)} copy(bf16[16,4096]{1,0:T(8,128)(2,1)} %get-tuple-element.4) | data formatting | bytes 262144
  30.2 0.0 copy-done
  30.2 0.7 %copy.14 = bf16[16,4096]{1,0:T(8,128)(2,1)} copy(bf16[16,4096]{1,0:T(8,128)(2,1)S(1)} %copy-done) | data formatting | bytes 262144
Async XLA Ops:
  28.6 1.6 %copy-start = (bf16[16,4096]{1,0:T(8,128)(2,1)S(1)}, bf16[16,4096]{1,0:T(8,128)(2,1)}, u32[]{:S(2)}) copy-start(bf16[16,4096]{1,0:T(8,128)(2,1)} %get-tuple-element.5) | copy-start | bytes 393220
